TPU v7x, 512 devices: a whole 4x4x16 slice. The times are simulated.
512 devices in a mesh: lat: 16 (over z_lo, core), lon: 32 (over x, z_hi, y).
Axes of the slice: x: 4, y: 4, z: 16 (z_hi: 2, z_lo: 8; z = z_hi * 8 + z_lo), core: 2. Of those that a mesh axis runs over, the one named last changes fastest.
Arguments:
- tokens: bfloat16 [192, 768, 512], P('lat', 'lon'), may hold values from -6 to 6
- fine_qkv: bfloat16 [512, 1536], P('lat'), may hold values from -0.25 to 0.25
- fine_out: bfloat16 [512, 512], P('lat'), may hold values from -0.25 to 0.25
- fine_scale: float32 [8], replicated, may hold values from 2 to 16
- fine_table: float32 [253, 8], replicated, may hold values from -3 to 3
- fine_gain: float32 [512], replicated, may hold values from 0.5 to 1.5
- merge_weight: bfloat16 [2048, 512], P('lat'), may hold values from -0.125 to 0.125
- merge_gain: float32 [512], replicated, may hold values from 0.5 to 1.5
- coarse_qkv: bfloat16 [512, 1536], P('lat'), may hold values from -0.25 to 0.25
- coarse_out: bfloat16 [512, 512], P('lat'), may hold values from -0.25 to 0.25
- coarse_scale: float32 [8], replicated, may hold values from 2 to 16
- coarse_table: float32 [253, 8], replicated, may hold values from -3 to 3
- coarse_gain: float32 [512], replicated, may hold values from 0.5 to 1.5
- shifts: int32 [2, 2], replicated, may hold values from 1 to 11, as said below
- bias_index: int32 [72, 72], replicated, may hold values from 0 to 252
Outputs:
- refined: bfloat16 [192, 768, 512], P('lat', 'lon')
Inputs may be any that keep to these rules, and one draw needn't show every extreme that they name: `shifts`: row 0 serves the fine level and row 1 the coarse one; the first entry of a row lies in 1 to 5, the second in 1 to 11; one level's row shift is 1 and one level's column shift is 11.
All inputs are finite; a program needn't handle non-finite values.
Results may differ from a plain program's by a relative error of at most 0.017.
Values may be sent and summed in bfloat16 or wider, within the bound.
A program may use at most 64 MiB of HBM per device.

v0:
```python
import jax
import jax.numpy as jnp
from jax import lax
from jax.sharding import PartitionSpec as P

HEADS = 8
HEADS2 = 8
WLAT = 6
WLON = 12


def padded(cells, sides, width, closed):
    for axis, dim in sides:
        count = lax.axis_size(axis)
        ends = count if closed else count - 1
        head = lax.slice_in_dim(cells, 0, width, axis=dim)
        tail = lax.slice_in_dim(cells, cells.shape[dim] - width, cells.shape[dim], axis=dim)
        cells = jnp.concatenate(
            [
                lax.ppermute(tail, axis, [(i, (i + 1) % count) for i in range(ends)]),
                cells,
                lax.ppermute(head, axis, [((i + 1) % count, i) for i in range(ends)]),
            ],
            axis=dim,
        )
    return cells


def layer_norm(values, gain):
    middle = jnp.mean(values, axis=-1, keepdims=True)
    centered = values - middle
    spread = jnp.mean(centered * centered, axis=-1, keepdims=True)
    return centered * lax.rsqrt(spread + 1e-05) * gain


def extend(field):
    wider = padded(field, (("lon", 1),), WLON - 1, True)
    return padded(wider, (("lat", 0),), WLAT - 1, False)


def windows_of(field):
    rows, columns, width = field.shape
    split = field.reshape(rows // WLAT, WLAT, columns // WLON, WLON, width)
    return split.transpose(0, 2, 1, 3, 4).reshape(-1, WLAT * WLON, width)


def from_windows(wins, rows, columns):
    width = wins.shape[-1]
    split = wins.reshape(rows // WLAT, columns // WLON, WLAT, WLON, width)
    return split.transpose(0, 2, 1, 3, 4).reshape(rows, columns, width)


def position_bias(table, bias_index):
    window = bias_index.shape[0]
    one_hot = (
        bias_index.reshape(-1, 1) == jnp.arange(table.shape[0], dtype=jnp.int32)[None, :]
    ).astype(jnp.float32)
    looked = jnp.dot(
        one_hot, table, precision=lax.Precision.HIGHEST, preferred_element_type=jnp.float32
    )
    return looked.reshape(window, window, -1).transpose(2, 0, 1)


def attend(query, keyval, keep, scale, bias, heads):
    number, window, width = query.shape
    depth = width // heads
    query_full = query.reshape(number, window, heads, depth).astype(jnp.float32)
    key_full = keyval[:, :, :width].reshape(number, window, heads, depth).astype(jnp.float32)
    value_half = keyval[:, :, width:].reshape(number, window, heads, depth)
    query_unit = query_full * lax.rsqrt(
        jnp.sum(query_full * query_full, axis=-1, keepdims=True) + 1e-06
    )
    key_unit = key_full * lax.rsqrt(jnp.sum(key_full * key_full, axis=-1, keepdims=True) + 1e-06)
    cosine = jnp.einsum(
        "nqhd,nkhd->nhqk",
        query_unit,
        key_unit,
        precision=lax.Precision.HIGHEST,
        preferred_element_type=jnp.float32,
    )
    scores = scale[None, :, None, None] * cosine + bias[None]
    powers = jnp.exp(scores) * keep[:, None, None, :]
    weights = (powers / jnp.sum(powers, axis=-1, keepdims=True)).astype(jnp.bfloat16)
    mixed = jnp.einsum("nhqk,nkhd->nqhd", weights, value_half, preferred_element_type=jnp.float32)
    return mixed.reshape(number, window, width).astype(jnp.bfloat16)


def sublayer(grid, w_qkv, w_out, scale, table, gain, shift, bias_index, heads):
    rows, columns, width = grid.shape
    flat = grid.reshape(-1, width)
    query = jnp.dot(flat, w_qkv[:, :width], preferred_element_type=jnp.float32).astype(jnp.bfloat16)
    wide = extend(grid)
    keyval = jnp.dot(
        wide.reshape(-1, width), w_qkv[:, width:], preferred_element_type=jnp.float32
    ).astype(jnp.bfloat16)
    keyval = keyval.reshape(wide.shape[0], wide.shape[1], 2 * width)
    shift_lat = shift[0]
    shift_lon = shift[1]
    span_rows = rows + WLAT
    span_columns = columns + WLON
    framed = lax.dynamic_slice(
        keyval, (shift_lat - 1, shift_lon - 1, 0), (span_rows, span_columns, 2 * width)
    )
    blank = jnp.zeros((span_rows, span_columns, width), jnp.bfloat16)
    placed = lax.dynamic_update_slice(
        blank, query.reshape(rows, columns, width), (WLAT - shift_lat, WLON - shift_lon, 0)
    )
    first_row = lax.axis_index("lat") * rows + shift_lat - WLAT
    latitude = first_row + jnp.arange(span_rows, dtype=jnp.int32)
    present = ((latitude >= 0) & (latitude < rows * lax.axis_size("lat"))).astype(jnp.float32)
    keep = windows_of(jnp.broadcast_to(present[:, None, None], (span_rows, span_columns, 1)))[
        :, :, 0
    ]
    bias = position_bias(table, bias_index)
    mixed = attend(windows_of(placed), windows_of(framed), keep, scale, bias, heads)
    mixed = from_windows(mixed, span_rows, span_columns)
    own = lax.dynamic_slice(mixed, (WLAT - shift_lat, WLON - shift_lon, 0), (rows, columns, width))
    branch = jnp.dot(own.reshape(-1, width), w_out, preferred_element_type=jnp.float32)
    result = flat.astype(jnp.float32) + layer_norm(branch, gain)
    return result.astype(jnp.bfloat16).reshape(rows, columns, width)


def per_device(
    tokens,
    fine_qkv,
    fine_out,
    fine_scale,
    fine_table,
    fine_gain,
    merge_weight,
    merge_gain,
    coarse_qkv,
    coarse_out,
    coarse_scale,
    coarse_table,
    coarse_gain,
    shifts,
    bias_index,
):
    whole_fine_qkv, whole_fine_out, whole_merge, whole_coarse_qkv, whole_coarse_out = (
        lax.all_gather(fine_qkv, "lat", axis=0, tiled=True),
        lax.all_gather(fine_out, "lat", axis=0, tiled=True),
        lax.all_gather(merge_weight, "lat", axis=0, tiled=True),
        lax.all_gather(coarse_qkv, "lat", axis=0, tiled=True),
        lax.all_gather(coarse_out, "lat", axis=0, tiled=True),
    )
    fine_after = sublayer(
        tokens,
        whole_fine_qkv,
        whole_fine_out,
        fine_scale,
        fine_table,
        fine_gain,
        shifts[0],
        bias_index,
        HEADS,
    )
    rows, columns, width = fine_after.shape
    quads = (
        fine_after.reshape(rows // 2, 2, columns // 2, 2, width)
        .transpose(0, 2, 3, 1, 4)
        .reshape(-1, 4 * width)
    )
    merged = jnp.dot(quads, whole_merge, preferred_element_type=jnp.float32)
    coarse = (
        layer_norm(merged, merge_gain).astype(jnp.bfloat16).reshape(rows // 2, columns // 2, -1)
    )
    coarse_after = sublayer(
        coarse,
        whole_coarse_qkv,
        whole_coarse_out,
        coarse_scale,
        coarse_table,
        coarse_gain,
        shifts[1],
        bias_index,
        HEADS2,
    )
    upward = jnp.repeat(jnp.repeat(coarse_after, 2, axis=0), 2, axis=1)
    return (fine_after.astype(jnp.float32) + upward.astype(jnp.float32)).astype(jnp.bfloat16)


def solution(mesh):
    placed = (
        P("lat", "lon", None),
        P("lat", None),
        P("lat", None),
        P(),
        P(),
        P(),
        P("lat", None),
        P(),
        P("lat", None),
        P("lat", None),
        P(),
        P(),
        P(),
        P(),
        P(),
    )
    return jax.shard_map(
        per_device, mesh=mesh, in_specs=placed, out_specs=P("lat", "lon", None), check_vma=False
    )
```

profile of v0, /device:TPU:1, one launch (start us, length us, event | category | flops | bytes accessed | tf_op | source)
XLA Modules:
  0.0 384.6 jit_solution(9279334041575351424)
XLA Ops:
  6.5 0.7 all-gather.4.cloned.1.call-update
  7.3 0.7 all-gather.6.cloned.1.call-update
  8.1 1.1 fusion.29
  9.2 4.0 %collective-permute-start = (bf16[12,11,512]{2,1,0:T(8,128)(2,1)S(1)}, bf16[12,11,512]{2,1,0:T(8,128)(2,1)S(1)}, u32[]{:S(2)}, u32[]{:S(2)}) collective-permute-start(bf16[12,11,512]{2,1,0:T(8,128)(2,1)S(1)} %get-tuple-element.11), channel_id=1, source_target_pairs={{0,1},{1,2},{2,3},{3,4},{4,5},{5,6},{6,7},{7,8},{8,9},{9,10},{10,1... | collective-permute-start | bytes 405512 | tf_op jit(solution)/shard_map/ppermute | solution.py:20
  13.2 18.8 %collective-permute-start.1 = (bf16[12,11,512]{2,1,0:T(8,128)(2,1)S(1)}, bf16[12,11,512]{2,1,0:T(8,128)(2,1)S(1)}, u32[]{:S(2)}, u32[]{:S(2)}) collective-permute-start(bf16[12,11,512]{2,1,0:T(8,128)(2,1)S(1)} %get-tuple-element.12), channel_id=1, source_target_pairs={{1,0},{2,1},{3,2},{4,3},{5,4},{6,5},{7,6},{8,7},{9,8},{10,9},{11,1... | collective-permute-start | bytes 405512 | tf_op jit(solution)/shard_map/ppermute | solution.py:22
  32.0 1.5 fusion.32
  42.1 0.9 eq.8
  42.9 2.5 fusion.1
  45.6 0.9 copy.110
  49.7 2.5 fusion
  52.4 0.8 copy.125
  53.2 38.1 %all_gather.16 = bf16[512,512]{1,0:T(8,128)(2,1)} all-gather(bf16[32,512]{1,0:T(8,128)(2,1)S(1)} %copy-done.14), channel_id=1, replica_groups=mesh['lat'=16,'lon'=32] {'lat'}, dimensions={0}, use_global_device_ids=true | all-gather | bytes 557056 | tf_op jit(solution)/shard_map/all_gather | solution.py:142
  91.4 1.9 collective-permute-start.2
  93.4 2.4 collective-permute-start.3
  95.8 30.4 %all_gather.19 = bf16[512,512]{1,0:T(8,128)(2,1)} all-gather(bf16[32,512]{1,0:T(8,128)(2,1)S(1)} %copy-done.15), channel_id=1, replica_groups=mesh['lat'=16,'lon'=32] {'lat'}, dimensions={0}, use_global_device_ids=true | all-gather | bytes 557056 | tf_op jit(solution)/shard_map/all_gather | solution.py:145
  126.7 3.8 convolution_convert_fusion
  130.5 2.5 reshape.225
  133.1 1.8 constant_dynamic-slice_fusion.3
  134.9 2.3 reshape.226
  137.7 1.5 slice_convert_fusion
  139.1 1.7 reshape.245
  140.8 0.8 multiply_reduce_fusion
  141.8 2.1 convolution_convert_fusion.4
  143.8 0.9 broadcast_in_dim.8
  144.7 3.5 dynamic_update_slice.6
  148.2 2.4 reshape.250
  150.6 3.0 copy.107
  153.6 3.2 reshape.244
  156.8 2.7 multiply_reduce_fusion.1
  159.6 1.8 broadcast_multiply_fusion
  161.5 6.8 %fusion.7 = (f32[9,8,72]{2,1,0:T(8,128)S(1)}, f32[9,8,72,72]{2,3,1,0:T(8,128)}) fusion(f32[9,72]{1,0:T(8,128)S(1)} %transpose.77, f32[8,72,72]{1,2,0:T(8,128)S(1)} %bitcast.72, f32[8]{0:T(128)S(1)} %copy-done.19, f32[9,72,8,64]{3,2,1,0:T(8,128)S(1)} %get-tuple-element.29, f32[9,72,8,64]{3,2,1,0:T(8,128)S(1)} %get-tuple-element.30), kind=kOutput, calls=%fused_computation.12 | convolution fusion | flops 288142272 | bytes 4336448 | tf_op jit(solution)/shard_map/nqhd,nkhd->nhqk/dot_general | solution.py:74
  168.3 0.9 copy.106
  169.2 3.8 fusion.11
  173.1 2.5 copy.112
  175.6 0.9 convert_element_type.141
  176.8 0.7 copy-done.11
  177.5 0.4 fusion.33
  179.0 41.7 %all-gather.6.cloned.1.call-done = bf16[2048,512]{1,0:T(8,128)(2,1)} async-done(((bf16[128,512]{1,0:T(8,128)(2,1)}), bf16[2048,512]{1,0:T(8,128)(2,1)}) %all-gather.6.cloned.1.call-update) | async-done | bytes 2097168 | tf_op jit(solution)/shard_map/all_gather | solution.py:143
  220.7 2.2 fusion.34
  223.1 0.5 copy-done.8
  223.7 99.4 %all-gather.8.cloned.1.call-done = bf16[512,1536]{1,0:T(8,128)(2,1)} async-done(((bf16[32,1536]{1,0:T(8,128)(2,1)}), bf16[512,1536]{1,0:T(8,128)(2,1)}) %all-gather.8.cloned.1.call-update) | async-done | bytes 1572880 | tf_op jit(solution)/shard_map/all_gather | solution.py:144
  323.1 1.2 convolution_convert_fusion.5
  324.8 0.5 copy.117
  325.3 0.6 reshape.247
  325.9 0.5 multiply_reduce_fusion.3
  326.6 3.2 collective-permute-start.4
  329.8 15.0 %collective-permute-start.5 = (bf16[6,11,512]{2,1,0:T(8,128)(2,1)S(1)}, bf16[6,11,512]{2,1,0:T(8,128)(2,1)S(1)}, u32[]{:S(2)}, u32[]{:S(2)}) collective-permute-start(bf16[6,11,512]{2,1,0:T(8,128)(2,1)S(1)} %get-tuple-element.16), channel_id=1, source_target_pairs={{1,0},{2,1},{3,2},{4,3},{5,4},{6,5},{7,6},{8,7},{9,8},{10,9},{11,1... | collective-permute-start | bytes 202760 | tf_op jit(solution)/shard_map/ppermute | solution.py:22
  344.9 1.5 collective-permute-done.5
  346.5 1.9 collective-permute-start.6
  348.5 4.3 %collective-permute-start.7 = (bf16[5,34,512]{2,1,0:T(8,128)(2,1)S(1)}, bf16[5,34,512]{2,1,0:T(8,128)(2,1)S(1)}, u32[]{:S(2)}, u32[]{:S(2)}) collective-permute-start(bf16[5,34,512]{2,1,0:T(8,128)(2,1)S(1)} %get-tuple-element.14), channel_id=1, source_target_pairs={{32,0},{64,32},{96,64},{128,96},{160,128},{192,160},{224,192},{256... | collective-permute-start | bytes 522248 | tf_op jit(solution)/shard_map/ppermute | solution.py:22
  353.1 3.5 collective-permute-done.7
  356.9 2.0 convolution_convert_fusion.2
  358.9 1.5 reshape.236
  360.4 1.3 constant_dynamic-slice_fusion.1
  361.8 0.6 copy.115
  362.7 0.9 fusion.28
  364.4 0.8 copy.122
  365.2 1.3 broadcast_multiply_fusion.2
  366.5 2.0 copy.116
  368.5 3.9 %fusion.10 = f32[4,8,72,72]{2,3,1,0:T(8,128)S(1)} fusion(f32[4,72,8,64]{3,2,1,0:T(8,128)S(1)} %broadcast_multiply_fusion.2, f32[4,72,8,64]{3,2,0,1:T(8,128)S(1)} %broadcast_multiply_fusion.3, f32[4,72]{1,0:T(4,128)S(1)} %transpose.83, f32[8,72,72]{1,2,0:T(8,128)} %bitcast.71, f32[8]{0:T(128)} %param.25), kind=kOutput, calls=%fused_computation.19 | convolution fusion | flops 127899648 | bytes 2010272 | tf_op jit(solution)/shard_map/nqhd,nkhd->nhqk/dot_general | solution.py:74
  372.4 1.4 fusion.12
  373.8 0.9 copy.127
  375.2 0.5 copy-done.10
  377.3 0.8 fusion.17
  (114 shorter events, 8.4 us)
Async XLA Ops:
  6.5 36.4 %copy-start = (f32[253,8]{0,1:T(8,128)S(1)}, f32[253,8]{0,1:T(8,128)}, u32[]{:S(2)}) copy-start(f32[253,8]{0,1:T(8,128)} %param.19) | copy-start | bytes 24292
  6.5 120.2 %all-gather.4.cloned.1.call-start = ((), (), s32[]{:S(2)}) async-start(), calls=%async_computation | async-start | bytes 1671168 | tf_op jit(solution)/shard_map/all_gather | solution.py:141
  7.3 213.4 %all-gather.6.cloned.1.call-start = ((), (), s32[]{:S(2)}) async-start(), calls=%async_computation.1 | async-start | bytes 2228224 | tf_op jit(solution)/shard_map/all_gather | solution.py:143
  8.0 315.1 %all-gather.8.cloned.1.call-start = ((), (), s32[]{:S(2)}) async-start(), calls=%async_computation.2 | async-start | bytes 1671168 | tf_op jit(solution)/shard_map/all_gather | solution.py:144
  9.1 40.5 %copy-start.20 = (f32[253,8]{0,1:T(8,128)S(1)}, f32[253,8]{0,1:T(8,128)}, u32[]{:S(2)}) copy-start(f32[253,8]{0,1:T(8,128)} %param.26) | copy-start | bytes 24292
  9.2 82.1 %collective-permute-start = (bf16[12,11,512]{2,1,0:T(8,128)(2,1)S(1)}, bf16[12,11,512]{2,1,0:T(8,128)(2,1)S(1)}, u32[]{:S(2)}, u32[]{:S(2)}) collective-permute-start(bf16[12,11,512]{2,1,0:T(8,128)(2,1)S(1)} %get-tuple-element.11), channel_id=1, source_target_pairs={{0,1},{1,2},{2,3},{3,4},{4,5},{5,6},{6,7},{7,8},{8,9},{9,10},{10,1... | collective-permute-start | bytes 405512 | tf_op jit(solution)/shard_map/ppermute | solution.py:20
  13.2 78.1 %collective-permute-start.1 = (bf16[12,11,512]{2,1,0:T(8,128)(2,1)S(1)}, bf16[12,11,512]{2,1,0:T(8,128)(2,1)S(1)}, u32[]{:S(2)}, u32[]{:S(2)}) collective-permute-start(bf16[12,11,512]{2,1,0:T(8,128)(2,1)S(1)} %get-tuple-element.12), channel_id=1, source_target_pairs={{1,0},{2,1},{3,2},{4,3},{5,4},{6,5},{7,6},{8,7},{9,8},{10,9},{11,1... | collective-permute-start | bytes 405512 | tf_op jit(solution)/shard_map/ppermute | solution.py:22
  45.6 7.6 %copy-start.14 = (bf16[32,512]{1,0:T(8,128)(2,1)S(1)}, bf16[32,512]{1,0:T(8,128)(2,1)}, u32[]{:S(2)}) copy-start(bf16[32,512]{1,0:T(8,128)(2,1)} %param.17) | copy-start | bytes 98308
  46.5 44.8 %copy-start.3 = (bf16[12,24,512]{2,1,0:T(8,128)(2,1)S(1)}, bf16[12,24,512]{2,1,0:T(8,128)(2,1)}, u32[]{:S(2)}) copy-start(bf16[12,24,512]{2,1,0:T(8,128)(2,1)} %param.15) | copy-start | bytes 884740
  52.2 43.6 %copy-start.15 = (bf16[32,512]{1,0:T(8,128)(2,1)S(1)}, bf16[32,512]{1,0:T(8,128)(2,1)}, u32[]{:S(2)}) copy-start(bf16[32,512]{1,0:T(8,128)(2,1)} %param.24) | copy-start | bytes 98308
  91.4 34.7 %collective-permute-start.2 = (bf16[5,46,512]{2,1,0:T(8,128)(2,1)S(1)}, bf16[5,46,512]{2,1,0:T(8,128)(2,1)S(1)}, u32[]{:S(2)}, u32[]{:S(2)}) collective-permute-start(bf16[5,46,512]{2,1,0:T(8,128)(2,1)S(1)} %get-tuple-element.7), channel_id=1, source_target_pairs={{0,32},{32,64},{64,96},{96,128},{128,160},{160,192},{192,224},{224... | collective-permute-start | bytes 706568 | tf_op jit(solution)/shard_map/ppermute | solution.py:20
  93.4 32.8 %collective-permute-start.3 = (bf16[5,46,512]{2,1,0:T(8,128)(2,1)S(1)}, bf16[5,46,512]{2,1,0:T(8,128)(2,1)S(1)}, u32[]{:S(2)}, u32[]{:S(2)}) collective-permute-start(bf16[5,46,512]{2,1,0:T(8,128)(2,1)S(1)} %get-tuple-element.8), channel_id=1, source_target_pairs={{32,0},{64,32},{96,64},{128,96},{160,128},{192,160},{224,192},{256... | collective-permute-start | bytes 706568 | tf_op jit(solution)/shard_map/ppermute | solution.py:22
  140.8 1.0 copy-start.4
  156.8 2.7 copy-start.2
  159.6 1.9 copy-start.12
  159.6 1.9 copy-start.19
  161.5 6.8 %copy-start.5 = (bf16[9,72,512]{2,1,0:T(8,128)(2,1)S(1)}, bf16[9,72,512]{2,1,0:T(8,128)(2,1)}, u32[]{:S(2)}) copy-start(bf16[9,72,512]{2,1,0:T(8,128)(2,1)} %get-tuple-element.6) | copy-start | bytes 1990660
  168.3 1.0 copy-start.13
  176.5 1.0 copy-start.11
  176.7 1.5 copy-start.17
  178.4 44.5 %copy-start.6 = (bf16[288,512]{1,0:T(8,128)(2,1)}, bf16[288,512]{1,0:T(8,128)(2,1)S(1)}, u32[]{:S(2)}) copy-start(bf16[288,512]{1,0:T(8,128)(2,1)S(1)} %add_convert_fusion) | copy-start | bytes 884740
  178.8 44.8 %copy-start.16 = (f32[512]{0:T(512)S(1)}, f32[512]{0:T(512)}, u32[]{:S(2)}) copy-start(f32[512]{0:T(512)} %param.22) | copy-start | bytes 6148
  222.9 0.7 copy-start.8
  326.6 18.4 %collective-permute-start.4 = (bf16[6,11,512]{2,1,0:T(8,128)(2,1)S(1)}, bf16[6,11,512]{2,1,0:T(8,128)(2,1)S(1)}, u32[]{:S(2)}, u32[]{:S(2)}) collective-permute-start(bf16[6,11,512]{2,1,0:T(8,128)(2,1)S(1)} %get-tuple-element.15), channel_id=1, source_target_pairs={{0,1},{1,2},{2,3},{3,4},{4,5},{5,6},{6,7},{7,8},{8,9},{9,10},{10,1... | collective-permute-start | bytes 202760 | tf_op jit(solution)/shard_map/ppermute | solution.py:20
  329.8 16.6 %collective-permute-start.5 = (bf16[6,11,512]{2,1,0:T(8,128)(2,1)S(1)}, bf16[6,11,512]{2,1,0:T(8,128)(2,1)S(1)}, u32[]{:S(2)}, u32[]{:S(2)}) collective-permute-start(bf16[6,11,512]{2,1,0:T(8,128)(2,1)S(1)} %get-tuple-element.16), channel_id=1, source_target_pairs={{1,0},{2,1},{3,2},{4,3},{5,4},{6,5},{7,6},{8,7},{9,8},{10,9},{11,1... | collective-permute-start | bytes 202760 | tf_op jit(solution)/shard_map/ppermute | solution.py:22
  346.5 6.6 %collective-permute-start.6 = (bf16[5,34,512]{2,1,0:T(8,128)(2,1)S(1)}, bf16[5,34,512]{2,1,0:T(8,128)(2,1)S(1)}, u32[]{:S(2)}, u32[]{:S(2)}) collective-permute-start(bf16[5,34,512]{2,1,0:T(8,128)(2,1)S(1)} %get-tuple-element.13), channel_id=1, source_target_pairs={{0,32},{32,64},{64,96},{96,128},{128,160},{160,192},{192,224},{224... | collective-permute-start | bytes 522248 | tf_op jit(solution)/shard_map/ppermute | solution.py:20
  348.5 8.1 %collective-permute-start.7 = (bf16[5,34,512]{2,1,0:T(8,128)(2,1)S(1)}, bf16[5,34,512]{2,1,0:T(8,128)(2,1)S(1)}, u32[]{:S(2)}, u32[]{:S(2)}) collective-permute-start(bf16[5,34,512]{2,1,0:T(8,128)(2,1)S(1)} %get-tuple-element.14), channel_id=1, source_target_pairs={{32,0},{64,32},{96,64},{128,96},{160,128},{192,160},{224,192},{256... | collective-permute-start | bytes 522248 | tf_op jit(solution)/shard_map/ppermute | solution.py:22
  374.6 1.0 copy-start.10
  374.7 1.5 copy-start.9
  374.7 1.5 copy-start.18
  376.3 1.0 copy-start.7
  376.4 1.7 copy-start.1
Sparse Core Ops, SparseCore 0:
  9.4 109.7 all-gather.3
  121.3 99.3 all-gather.5
  222.8 100.3 all-gather.7
where the time goes:
time: 390 us; the launch traced here: 385 us
  waiting for transfers between devices  148 us (38%)
  blocking collectives  68.5 us (18%)
  starting transfers between devices  51.6 us (13%)
  local copies, waits for them, and re-layouts  47 us (12%)
  matrix products  32.8 us (8%)
  between operations  25.4 us (7%)
  other arithmetic  11.8 us (3%)
    all_gather x1, waiting for transfers between devices, per_device(): lax.all_gather(coarse_qkv, 'lat', axis=0, tiled=True)  99.4 us
    all_gather x1, waiting for transfers between devices, per_device(): lax.all_gather(merge_weight, 'lat', axis=0, tiled=True)  41.7 us
    ppermute x4, starting transfers between devices, padded(): lax.ppermute(head, axis, [((i + 1) % count, i) for i in range(ends)])  40.5 us
    all_gather x1, blocking collectives, per_device(): lax.all_gather(fine_out, 'lat', axis=0, tiled=True)  38.1 us
    all_gather x1, blocking collectives, per_device(): lax.all_gather(coarse_out, 'lat', axis=0, tiled=True)  30.4 us
    ppermute x4, starting transfers between devices, padded(): lax.ppermute(tail, axis, [(i, (i + 1) % count) for i in range(ends)])  11.1 us
    dot_general x2, matrix products, attend(): jnp.einsum('nqhd,nkhd->nhqk', query_unit, key_unit, precision=lax.Precisi...  10.7 us
    convert_element_type x6, local copies, waits for them, and re-layouts, attend(): query_full = query.reshape(number, window, heads, depth).astype(jnp.float32)  9.73 us
  transfers between devices with their start and end apart: 11, of which 4 were waited for; matrix products, arithmetic and copies ran while one was open for 17% of the time, Pallas kernels for 0%

commit v1 on v0

v1 whole, which is shorter than its diff:
```python
import functools

import jax
import jax.numpy as jnp
import numpy as np
from jax import lax
from jax.experimental import pallas as pl
from jax.experimental.pallas import tpu as pltpu
from jax.sharding import PartitionSpec as P

MESH = pl.DeviceIdType.MESH
HEADS = 8
WLAT = 6
WLON = 12
WIN = 72
PAD = 80
D = 512
BF = jnp.bfloat16
F32 = jnp.float32

OWN, LEFT, RIGHT = 0, 288, 432
ABOVE, ABOVE_C, BELOW, BELOW_C = 576, 704, 816, 944
POOL = 1056
CPOOL = 720
NOWHERE = -200000
UNUSED = -100000


def code(row, column):
    return (row + 32) * 128 + column + 32


def padded_codes(places, length, fill):
    out = np.full((length,), fill, np.int32)
    out[: len(places)] = [code(r, c) for r, c in places]
    return out


def grid_places(rows, columns):
    return [(r, c) for r in rows for c in columns]


def frame_places(down, across):
    parts = []
    for a in range(down):
        for b in range(across):
            rows = range(WLAT * a - WLAT, WLAT * a)
            columns = range(WLON * b - WLON, WLON * b)
            parts.append(grid_places(rows, columns))
    return parts


def blocks_of(parts, block, fill):
    return np.concatenate([padded_codes(p, block, fill) for p in parts])


def code_tables():
    own = grid_places(range(12), range(24))
    far_left = grid_places(range(12), range(-11, 0))
    far_right = grid_places(range(12), range(24, 35))
    sides = list(range(-11, 0)) + list(range(24, 35))
    above, below = range(-5, 0), range(12, 17)
    pool = np.concatenate(
        [
            padded_codes(own, 288, NOWHERE),
            padded_codes(far_left, 144, NOWHERE),
            padded_codes(far_right, 144, NOWHERE),
            padded_codes(grid_places(above, range(24)), 128, NOWHERE),
            padded_codes(grid_places(above, sides), 112, NOWHERE),
            padded_codes(grid_places(below, range(24)), 128, NOWHERE),
            padded_codes(grid_places(below, sides), 112, NOWHERE),
        ]
    )
    quads = [
        [(2 * a + i, 2 * b + j) for a in range(6) for b in range(12)]
        for j in range(2)
        for i in range(2)
    ]
    coarse_pool = [
        grid_places(range(6 * down, 6 * down + 6), range(12 * across, 12 * across + 12))
        for down in (0, -1, 1)
        for across in (0, -1, 1)
    ]
    fine_frame, coarse_frame = frame_places(3, 3), frame_places(2, 2)
    by_row = np.full((8, 1152), NOWHERE, np.int32)
    for at, values in enumerate(
        [
            pool,
            blocks_of(fine_frame, PAD, NOWHERE),
            blocks_of(quads, PAD, NOWHERE),
            blocks_of(coarse_pool, PAD, NOWHERE),
            blocks_of(coarse_frame, PAD, NOWHERE),
        ]
    ):
        by_row[at, : len(values)] = values
    by_column = np.full((720, 128), UNUSED, np.int32)
    for at, values in enumerate(
        [
            blocks_of(fine_frame, PAD, UNUSED),
            blocks_of(quads, PAD, UNUSED),
            blocks_of(coarse_frame, PAD, UNUSED),
            blocks_of([grid_places(range(6), range(12))], PAD, UNUSED),
            padded_codes(own, 288, UNUSED),
            padded_codes(grid_places(range(12), range(13, 24)), 144, UNUSED),
            padded_codes(grid_places(range(12), range(11)), 144, UNUSED),
            padded_codes(grid_places(range(7, 12), range(24)), 128, UNUSED),
            padded_codes(grid_places(range(5), range(24)), 128, UNUSED),
            padded_codes(grid_places(range(7, 12), sides), 112, UNUSED),
            padded_codes(grid_places(range(5), sides), 112, UNUSED),
        ]
    ):
        by_column[: len(values), at] = values
    return by_row, by_column


def norm_rows(values, gain):
    middle = jnp.mean(values, axis=-1, keepdims=True)
    centered = values - middle
    spread = jnp.mean(centered * centered, axis=-1, keepdims=True)
    return centered * lax.rsqrt(spread + 1e-05) * gain


def dot(a, b):
    return jnp.dot(a, b, preferred_element_type=F32)


def dot_nt(a, b):
    return lax.dot_general(a, b, (((1,), (1,)), ((), ())), preferred_element_type=F32)


def kernel(
    shifts,
    fine_scale,
    coarse_scale,
    tokens,
    w_fine_qkv,
    w_fine_out,
    w_merge,
    w_coarse_qkv,
    w_coarse_out,
    tables,
    bias_index,
    gains,
    by_row,
    by_column,
    out,
    fine_qkv,
    fine_out,
    merge,
    coarse_qkv,
    coarse_out,
    pool,
    to_right,
    to_left,
    to_below,
    to_above,
    to_below_c,
    to_above_c,
    query,
    key,
    value,
    mixed,
    fine_after,
    coarse_pool,
    bias,
    send_sem,
    recv_sem,
    local_sem,
):
    lat, lon = lax.axis_index("lat"), lax.axis_index("lon")
    core, z_lo = lat % 2, lat // 2
    x, z_hi, y = lon // 8, (lon // 4) % 2, lon % 4
    z = z_hi * 8 + z_lo

    def place(x, y, z, core):
        x, y, z = (x + 4) % 4, (y + 4) % 4, (z + 16) % 16
        return ((z % 8) * 2 + core, x * 8 + (z // 8) * 4 + y)

    def along_z(d):
        return place(x, y, z + d, core)

    def along_x(d):
        return place(x + d, y, z, core)

    def along_y(d):
        return place(x, y + d, z, core)

    line = z * 2 + core

    def along_lat(d):
        spot = (line + d + 32) % 32
        return place(x, y, spot // 2, spot % 2)

    def along_lon(d):
        return (lat, (lon + d + 32) % 32)

    sibling = place(x, y, z, 1 - core)
    opposite = 4 - 8 * core
    hops = (opposite, 3, -3, 2, -2, 1, -1)

    barrier = pltpu.get_barrier_semaphore()
    senders = [along_z(-d) for d in hops]
    senders += [along_x(d) for d in (1, -1, 2)] + [along_y(d) for d in (1, -1, 2)]
    senders += [sibling, along_lon(1), along_lon(-1), along_lat(1), along_lat(-1)]
    for device in senders:
        pl.semaphore_signal(barrier, inc=1, device_id=device, device_id_type=MESH)

    def picked(column, rows, row_at, first, width, offset=0):
        left = by_column[0:rows, column : column + 1] + offset
        right = by_row[row_at : row_at + 1, first : first + width]
        return jnp.where(left == right, 1.0, 0.0).astype(BF)

    own = tokens[...]
    to_right[...] = dot(picked(5, 144, 0, OWN, 288), own).astype(BF)
    to_left[...] = dot(picked(6, 144, 0, OWN, 288), own).astype(BF)
    to_below[...] = dot(picked(7, 128, 0, OWN, 288), own).astype(BF)
    to_above[...] = dot(picked(8, 128, 0, OWN, 288), own).astype(BF)
    pool[OWN : OWN + 288, :] = own

    table = tables[...]
    top = table.astype(BF)
    rest = table - top.astype(F32)
    middle = rest.astype(BF)
    bottom = (rest - middle.astype(F32)).astype(BF)
    table_parts = jnp.concatenate([top, middle, bottom], axis=0)
    levels = lax.broadcasted_iota(jnp.int32, (256, 128), 0)

    def bias_rows(group, carry):
        rows = bias_index[pl.ds(pl.multiple_of(group * 8, 8), 8), :]
        for i in range(8):
            hot = jnp.where(levels == rows[i : i + 1, :], 1.0, 0.0).astype(BF)
            parts = dot(table_parts, hot)
            looked = parts[0:16] + parts[16:32] + parts[32:48]
            bias[:, pl.ds(group * 8 + i, 1), :] = looked.reshape(16, 1, 128)
        return carry

    lax.fori_loop(0, PAD // 8, bias_rows, 0)

    counter = [0]
    sent = []

    def send(source, target, device):
        at = counter[0]
        counter[0] += 1
        copy = pltpu.make_async_remote_copy(
            src_ref=source,
            dst_ref=target,
            send_sem=send_sem.at[at],
            recv_sem=recv_sem.at[at],
            device_id=device,
            device_id_type=MESH,
        )
        copy.start()
        sent.append(copy)
        return copy

    def arrived(copies):
        for copy in copies:
            copy.wait_recv()

    pl.semaphore_wait(barrier, len(senders))

    side_copies = [
        send(to_right, pool.at[pl.ds(LEFT, 144)], along_lon(1)),
        send(to_left, pool.at[pl.ds(RIGHT, 144)], along_lon(-1)),
    ]
    row_copies = [
        send(to_below, pool.at[pl.ds(ABOVE, 128)], along_lat(1)),
        send(to_above, pool.at[pl.ds(BELOW, 128)], along_lat(-1)),
    ]

    def corner(g, first, width):
        rows = pl.ds(pl.multiple_of((g // 2) * 16, 16), 16)
        return rows, pl.ds(pl.multiple_of(first + (g % 2) * width, 128), width)

    def band(g, first, width):
        return pl.ds(pl.multiple_of(g * 32, 32), 32), pl.ds(first, width)

    local_count = [0]

    class Gather:
        def __init__(self, shard, whole, halves):
            self.shard, self.whole, self.halves = shard, whole, halves

        def start(self):
            self.own, self.first = [], []
            for axis, (rows, columns) in self.halves:
                at = local_count[0]
                local_count[0] += 1
                copy = pltpu.make_async_copy(
                    self.shard.at[rows, columns],
                    self.whole.at[z_lo, core, rows, columns],
                    local_sem.at[at],
                )
                copy.start()
                self.own.append(copy)
                for d in hops:
                    self.first.append(
                        send(
                            self.shard.at[rows, columns],
                            self.whole.at[z_lo, core, rows, columns],
                            along_z(d),
                        )
                    )

        def spread(self):
            for copy in self.own:
                copy.wait()
            arrived(self.first)
            self.second = []
            for axis, (rows, columns) in self.halves:
                for d in (1, -1, 2):
                    part = self.whole.at[:, core, rows, columns]
                    self.second.append(send(part, part, axis(d)))

        def share(self):
            arrived(self.second)
            part = self.whole.at[:, core]
            self.third = [send(part, part, sibling)]

        def finish(self):
            arrived(self.third)

    wide_halves = [(along_x, corner(x, 0, 384)), (along_y, corner(y, 768, 384))]
    g_fine_qkv = Gather(w_fine_qkv, fine_qkv, wide_halves)
    g_fine_out = Gather(w_fine_out, fine_out, [(along_x, corner(x, 0, 256))])
    g_merge = Gather(w_merge, merge, [(along_x, band(x, 0, 256)), (along_y, band(y, 256, 256))])
    g_coarse_qkv = Gather(w_coarse_qkv, coarse_qkv, wide_halves)
    g_coarse_out = Gather(w_coarse_out, coarse_out, [(along_y, corner(y, 0, 256))])

    g_fine_qkv.start()
    g_fine_out.start()
    g_merge.start()
    g_fine_qkv.spread()
    g_fine_qkv.share()
    g_fine_out.spread()
    g_merge.spread()

    arrived(side_copies)
    sides = pool[LEFT : LEFT + 288, :]
    own_sides = pool[OWN : OWN + 576, :]
    to_below_c[...] = dot(picked(9, 112, 0, OWN, 576), own_sides).astype(BF)
    to_above_c[...] = dot(picked(10, 112, 0, OWN, 576), own_sides).astype(BF)
    row_copies += [
        send(to_below_c, pool.at[pl.ds(ABOVE_C, 112)], along_lat(1)),
        send(to_above_c, pool.at[pl.ds(BELOW_C, 112)], along_lat(-1)),
    ]
    g_fine_out.share()
    g_merge.share()
    g_coarse_qkv.start()
    g_coarse_out.start()

    lane = lax.broadcasted_iota(jnp.int32, (1, 128), 1)
    low = jnp.where(lane < 64, 1.0, 0.0).astype(BF)
    high = jnp.where(lane < 64, 0.0, 1.0).astype(BF)
    row_of = jnp.zeros((1, 128), jnp.int32)
    for r in range(1, WLAT):
        row_of = row_of + jnp.where(lane >= WLON * r, 1, 0)
    ones_row = lax.broadcasted_iota(jnp.int32, (256, 256), 0) // 64
    ones_column = lax.broadcasted_iota(jnp.int32, (256, 256), 1) // 64
    same_head = jnp.where(ones_row == ones_column, 1.0, 0.0).astype(BF)

    def scale_row(scale):
        head_of = lax.broadcasted_iota(jnp.int32, (1, D), 1) // 64
        row = jnp.zeros((1, D), F32)
        for n in range(HEADS):
            row = jnp.where(head_of == n, scale[n], row)
        return row

    def project(level, across, down, column, row_at, cells, width, weights, scale):
        offset = shifts[level, 0] * 128 + shifts[level, 1]
        scales = scale_row(scale)
        tall = across * PAD

        def one(a, carry):
            at = pl.multiple_of(a * tall, tall)
            left = by_column[pl.ds(at, tall), column : column + 1] + offset
            right = by_row[row_at : row_at + 1, 0:width]
            hot = jnp.where(left == right, 1.0, 0.0).astype(BF)
            frame = dot(hot, cells[...]).astype(BF)
            for n in range(6):
                block = weights[:, :, :, 256 * n : 256 * n + 256].reshape(D, 256)
                rounded = dot(frame, block).astype(BF)
                where_to = pl.ds(a * across, across)
                columns = slice(256 * (n % 2), 256 * (n % 2) + 256)
                if n < 4:
                    full = rounded.astype(F32)
                    square = dot((full * full).astype(BF), same_head)
                    full = full * lax.rsqrt(square + 1e-06)
                    if n < 2:
                        full = full * scales[:, columns]
                    rounded = full.astype(BF)
                target = (query, key, value)[n // 2]
                target[where_to, :, columns] = rounded.reshape(across, PAD, 256)
            return carry

        lax.fori_loop(0, down, one, 0)

    def attend(level, across, down, rows_here):
        first_row = lat * rows_here + shifts[level, 0] - WLAT

        def one(w, carry):
            latitude = row_of + (first_row + WLAT * (w // across))
            here = (latitude >= 0) & (latitude < rows_here * 16) & (lane < WIN)
            keep = jnp.where(here, 1.0, 0.0)[:, 0:PAD]
            for p in range(HEADS // 2):
                columns = slice(128 * p, 128 * p + 128)
                q = query[w, :, columns]
                pair = jnp.concatenate([q * low, q * high], axis=0)
                scores = dot_nt(pair, key[w, :, columns])
                own_bias = bias[8 * level + 2 * p : 8 * level + 2 * p + 2, :, 0:PAD]
                powers = jnp.exp(scores + own_bias.reshape(2 * PAD, PAD)) * keep
                total = jnp.sum(powers, axis=-1, keepdims=True)
                weights = (powers * (1.0 / total)).astype(BF)
                both = dot(weights, value[w, :, columns])
                taken = jnp.where(lane < 64, both[0:PAD], both[PAD : 2 * PAD])
                mixed[w, :, columns] = taken.astype(BF)
            return carry

        lax.fori_loop(0, across * down, one, 0)

    def finish(level, windows, column, rows, row_at, weights, base, gain):
        offset = shifts[level, 0] * 128 + shifts[level, 1]
        left = by_column[0:rows, column : column + 1] - offset
        right = by_row[row_at : row_at + 1, 0 : windows * PAD]
        hot = jnp.where(left == right, 1.0, 0.0).astype(BF)
        taken = dot(hot, mixed[0:windows].reshape(windows * PAD, D)).astype(BF)
        branch = dot(taken, weights[...].reshape(D, D))
        return (base + norm_rows(branch, gain)).astype(BF)

    g_fine_qkv.finish()
    arrived(row_copies)
    project(0, 3, 3, 0, 0, pool, POOL, fine_qkv, fine_scale)
    attend(0, 3, 3, 12)
    g_coarse_qkv.spread()
    g_coarse_out.spread()
    g_fine_out.finish()
    in_quads = dot(picked(1, 320, 0, OWN, 288), tokens[...])
    fine_after[...] = finish(0, 9, 1, 320, 1, fine_out, in_quads, gains[0:1, :])
    g_merge.finish()
    merged = jnp.zeros((PAD, D), F32)
    for p in range(4):
        rows = merge[2 * p : 2 * p + 2].reshape(D, D)
        merged = merged + dot(fine_after[PAD * p : PAD * p + PAD, :], rows)
    coarse_pool[0:PAD, :] = norm_rows(merged, gains[1:2, :]).astype(BF)
    mine = coarse_pool.at[pl.ds(0, PAD)]
    side_copies = [
        send(mine, coarse_pool.at[pl.ds(PAD, PAD)], along_lon(1)),
        send(mine, coarse_pool.at[pl.ds(2 * PAD, PAD)], along_lon(-1)),
    ]
    g_coarse_qkv.share()
    g_coarse_out.share()
    arrived(side_copies)
    three = coarse_pool.at[pl.ds(0, 3 * PAD)]
    row_copies = [
        send(three, coarse_pool.at[pl.ds(3 * PAD, 3 * PAD)], along_lat(1)),
        send(three, coarse_pool.at[pl.ds(6 * PAD, 3 * PAD)], along_lat(-1)),
    ]
    g_coarse_qkv.finish()
    arrived(row_copies)
    project(1, 2, 2, 2, 3, coarse_pool, CPOOL, coarse_qkv, coarse_scale)
    attend(1, 2, 2, 6)
    g_coarse_out.finish()
    base = coarse_pool[0:PAD, :].astype(F32)
    coarse_after = finish(1, 4, 3, PAD, 4, coarse_out, base, gains[2:3, :]).astype(F32)
    for p in range(4):
        part = fine_after[PAD * p : PAD * p + PAD, :].astype(F32) + coarse_after
        fine_after[PAD * p : PAD * p + PAD, :] = part.astype(BF)
    out[...] = dot(picked(4, 288, 2, 0, 320), fine_after[...]).astype(BF)
    for copy in sent:
        copy.wait_send()


COPIES = 4 + 2 + 4 + 3 * 21 + 2 * 11


def per_device(
    tokens,
    fine_qkv,
    fine_out,
    fine_scale,
    fine_table,
    fine_gain,
    merge_weight,
    merge_gain,
    coarse_qkv,
    coarse_out,
    coarse_scale,
    coarse_table,
    coarse_gain,
    shifts,
    bias_index,
):
    by_row, by_column = code_tables()
    tables = jnp.concatenate([fine_table, coarse_table], axis=1)
    tables = jnp.pad(tables, ((0, 3), (0, 0))).T
    index = jnp.pad(bias_index, ((0, 8), (0, 56)), constant_values=255)
    gains = jnp.stack([fine_gain, merge_gain, coarse_gain])
    rows, columns, width = tokens.shape
    smem = pl.BlockSpec(memory_space=pltpu.SMEM)
    vmem = pl.BlockSpec(memory_space=pltpu.VMEM)
    anywhere = pl.BlockSpec(memory_space=pl.ANY)
    result = pl.pallas_call(
        kernel,
        out_shape=jax.ShapeDtypeStruct((rows * columns, width), BF),
        in_specs=[smem] * 3 + [vmem] + [anywhere] * 5 + [vmem] * 5,
        out_specs=vmem,
        scratch_shapes=[
            pltpu.VMEM((8, 2, 32, 1536), BF),
            pltpu.VMEM((8, 2, 32, 512), BF),
            pltpu.VMEM((8, 2, 128, 512), BF),
            pltpu.VMEM((8, 2, 32, 1536), BF),
            pltpu.VMEM((8, 2, 32, 512), BF),
            pltpu.VMEM((POOL, D), BF),
            pltpu.VMEM((144, D), BF),
            pltpu.VMEM((144, D), BF),
            pltpu.VMEM((128, D), BF),
            pltpu.VMEM((128, D), BF),
            pltpu.VMEM((112, D), BF),
            pltpu.VMEM((112, D), BF),
            pltpu.VMEM((9, PAD, D), BF),
            pltpu.VMEM((9, PAD, D), BF),
            pltpu.VMEM((9, PAD, D), BF),
            pltpu.VMEM((9, PAD, D), BF),
            pltpu.VMEM((320, D), BF),
            pltpu.VMEM((CPOOL, D), BF),
            pltpu.VMEM((16, PAD, 128), F32),
            pltpu.SemaphoreType.DMA((COPIES,)),
            pltpu.SemaphoreType.DMA((COPIES,)),
            pltpu.SemaphoreType.DMA((8,)),
        ],
        compiler_params=pltpu.CompilerParams(
            collective_id=0, has_side_effects=True, vmem_limit_bytes=48 << 20
        ),
    )(
        shifts,
        fine_scale,
        coarse_scale,
        tokens.reshape(rows * columns, width),
        fine_qkv,
        fine_out,
        merge_weight,
        coarse_qkv,
        coarse_out,
        tables,
        index,
        gains,
        jnp.asarray(by_row),
        jnp.asarray(by_column),
    )
    return result.reshape(rows, columns, width)


def solution(mesh):
    placed = (
        P("lat", "lon", None),
        P("lat", None),
        P("lat", None),
        P(),
        P(),
        P(),
        P("lat", None),
        P(),
        P("lat", None),
        P("lat", None),
        P(),
        P(),
        P(),
        P(),
        P(),
    )
    return jax.shard_map(
        per_device, mesh=mesh, in_specs=placed, out_specs=P("lat", "lon", None), check_vma=False
    )
```

time: 390 us -> 103 us (0.26); the launches traced: 385 us -> 102 us
  waiting for transfers between devices: 148 us -> 0 us
  Pallas kernels: 0 us -> 93.1 us
  blocking collectives: 68.5 us -> 0 us
  starting transfers between devices: 51.6 us -> 0 us
  local copies, waits for them, and re-layouts: 47 us -> 7.55 us
  matrix products: 32.8 us -> 0 us
  between operations: 25.4 us -> 0.06 us
  other arithmetic: 11.8 us -> 1.49 us
    all_gather x3 -> x0, waiting for transfers between devices: 141 us -> none  [the longest x1 99.4 us: per_device(): lax.all_gather(coarse_qkv, 'lat', axis=0, tiled=True)]
    pallas_call x0 -> x1, Pallas kernels: none -> 93.1 us  [per_device(): pl.pallas_call(kernel, out_shape=jax.ShapeDtypeStruct((rows * columns, wi...]
    all_gather x2 -> x0, blocking collectives: 68.5 us -> none  [the longest x1 38.1 us: per_device(): lax.all_gather(fine_out, 'lat', axis=0, tiled=True)]
    ppermute x8 -> x0, starting transfers between devices: 51.6 us -> none  [the longest x4 40.5 us: padded(): lax.ppermute(head, axis, [((i + 1) % count, i) for i in range(ends)])]
    dot_general x13 -> x0, matrix products: 32.8 us -> none  [the longest x2 10.7 us: attend(): jnp.einsum('nqhd,nkhd->nhqk', query_unit, key_unit, precision=lax.Precisi...]
    convert_element_type x14 -> x0, local copies, waits for them, and re-layouts: 16.6 us -> none  [the longest x6 9.73 us: attend(): query_full = query.reshape(number, window, heads, depth).astype(jnp.float32)]
    reshape x18 -> x0, local copies, waits for them, and re-layouts: 9.91 us -> none  [the longest x2 4.06 us: sublayer(): keyval = keyval.reshape(wide.shape[0], wide.shape[1], 2 * width)]
    slice x7 -> x0, local copies, waits for them, and re-layouts: 6.53 us -> none  [the longest x2 2.97 us: attend(): value_half = keyval[:, :, width:].reshape(number, window, heads, depth)]
  transfers between devices with their start and end apart: 11 -> 0, of which waited for: 4 -> 0; matrix products, arithmetic and copies ran while one was open for 17% -> 0% of each run, Pallas kernels for 0% -> 0%
where the time goes in v1:
time: 103 us; the launch traced here: 102 us
  Pallas kernels  93.1 us (90%)
  local copies, waits for them, and re-layouts  7.55 us (7%)
  other arithmetic  1.49 us (1%)
    pallas_call x1, Pallas kernels, per_device(): pl.pallas_call(kernel, out_shape=jax.ShapeDtypeStruct((rows * columns, wi...  93.1 us
    unnamed x23, local copies, waits for them, and re-layouts  6.74 us

profile of v1, /device:TPU:1, one launch (start us, length us, event | category | flops | bytes accessed | tf_op | source)
XLA Modules:
  0.0 102.2 jit_solution(3805033253029347738)
XLA Ops:
  0.0 0.0 copy-start.2
  0.0 0.8 pad_maximum_fusion.gains
  0.8 0.7 fusion.tables
  1.5 0.0 copy-start.8
  1.5 0.0 copy-start.9
  1.5 0.0 copy-start.10
  1.5 0.8 pad.9.bias_index
  2.3 0.0 copy-done.2
  2.3 0.0 copy-done.8
  2.3 0.0 copy-done.9
  2.3 0.0 copy-done.10
  2.3 0.0 copy-start
  2.4 1.0 copy-done
  3.3 0.0 copy-start.1
  3.3 1.0 copy-done.1
  4.3 0.0 copy-start.3
  4.3 0.9 copy-done.3
  5.2 0.0 copy-start.4
  5.2 0.9 copy-done.4
  6.1 0.0 copy-start.5
  6.1 0.8 copy-done.5
  6.9 0.0 copy-start.6
  6.9 0.8 copy-done.6
  7.6 0.0 copy-start.7
  7.6 0.8 copy-done.7
  8.4 93.1 %shard_map.163 = bf16[288,512]{1,0:T(8,128)(2,1)S(1)} custom-call(s32[2,2]{1,0:T(2,128)S(1)} %copy-done.8, f32[8]{0:T(128)S(1)} %copy-done.9, f32[8]{0:T(128)S(1)} %copy-done.10, bf16[288,512]{1,0:T(8,128)(2,1)S(1)} %bitcast.8, bf16[32,1536]{1,0:T(8,128)(2,1)S(1)} %copy-done.3, bf16[32,512]{1,0:T(8,128)(2,1)S(1)} %copy-done.6, ...), custom_call_target="tpu_custom_call" | custom-call | tf_op jit(solution)/shard_map/pallas_call | solution.py:503
  101.5 0.7 copy.19
Async XLA Ops:
  0.0 2.3 %copy-start.2 = (bf16[128,512]{1,0:T(8,128)(2,1)S(1)}, bf16[128,512]{1,0:T(8,128)(2,1)}, u32[]{:S(2)}) copy-start(bf16[128,512]{1,0:T(8,128)(2,1)} %w_merge.1) | copy-start | bytes 393220
  1.5 0.8 copy-start.8
  1.5 0.8 copy-start.9
  1.5 0.8 copy-start.10
  2.3 1.0 copy-start
  3.3 1.0 copy-start.1
  4.3 0.9 copy-start.3
  5.2 0.9 copy-start.4
  6.1 0.8 copy-start.5
  6.9 0.8 copy-start.6
  7.6 0.8 copy-start.7

commit v2 on v1

v2 whole, which is shorter than its diff:
```python
import functools

import jax
import jax.numpy as jnp
import numpy as np
from jax import lax
from jax.experimental import pallas as pl
from jax.experimental.pallas import tpu as pltpu
from jax.sharding import PartitionSpec as P

MESH = pl.DeviceIdType.MESH
HEADS = 8
WLAT = 6
WLON = 12
WIN = 72
PAD = 80
D = 512
BF = jnp.bfloat16
F32 = jnp.float32

ABOVE, BELOW, OWN, LEFT, RIGHT, ABOVE_C, BELOW_C = 0, 128, 256, 544, 688, 832, 944
POOL = 1056
C_LEFT, C_RIGHT, C_ABOVE, C_BELOW, C_ABOVE_C, C_BELOW_C = 80, 160, 240, 320, 400, 512
CPOOL = 624
FINE_WINDOWS = [(0, 1), (1, 1), (2, 1), (1, 0), (1, 2), (0, 0), (0, 2), (2, 0), (2, 2)]
COARSE_WINDOWS = [(0, 0), (0, 1), (1, 0), (1, 1)]
NOWHERE = -200000
UNUSED = -100000


def code(row, column):
    return (row + 32) * 128 + column + 32


def padded_codes(places, length, fill):
    out = np.full((length,), fill, np.int32)
    out[: len(places)] = [code(r, c) for r, c in places]
    return out


def grid_places(rows, columns):
    return [(r, c) for r in rows for c in columns]


def frame_places(windows):
    parts = []
    for a, b in windows:
        rows = range(WLAT * a - WLAT, WLAT * a)
        columns = range(WLON * b - WLON, WLON * b)
        parts.append(grid_places(rows, columns))
    return parts


def blocks_of(parts, block, fill):
    return np.concatenate([padded_codes(p, block, fill) for p in parts])


def code_tables():
    own = grid_places(range(12), range(24))
    far_left = grid_places(range(12), range(-11, 0))
    far_right = grid_places(range(12), range(24, 35))
    sides = list(range(-11, 0)) + list(range(24, 35))
    above, below = range(-5, 0), range(12, 17)
    pool = np.concatenate(
        [
            padded_codes(grid_places(above, range(24)), 128, NOWHERE),
            padded_codes(grid_places(below, range(24)), 128, NOWHERE),
            padded_codes(own, 288, NOWHERE),
            padded_codes(far_left, 144, NOWHERE),
            padded_codes(far_right, 144, NOWHERE),
            padded_codes(grid_places(above, sides), 112, NOWHERE),
            padded_codes(grid_places(below, sides), 112, NOWHERE),
        ]
    )
    quads = [
        [(2 * a + i, 2 * b + j) for a in range(6) for b in range(12)]
        for j in range(2)
        for i in range(2)
    ]
    coarse_sides = list(range(-11, 0)) + list(range(12, 23))
    coarse_tiles = [(0, 0), (0, -1), (0, 1), (-1, 0), (1, 0)]
    coarse_pool = np.concatenate(
        [
            padded_codes(
                grid_places(range(6 * i, 6 * i + 6), range(12 * j, 12 * j + 12)), PAD, NOWHERE
            )
            for i, j in coarse_tiles
        ]
        + [
            padded_codes(grid_places(range(-5, 0), coarse_sides), 112, NOWHERE),
            padded_codes(grid_places(range(6, 11), coarse_sides), 112, NOWHERE),
        ]
    )
    fine_frame, coarse_frame = frame_places(FINE_WINDOWS), frame_places(COARSE_WINDOWS)
    by_row = np.full((8, 1152), NOWHERE, np.int32)
    for at, values in enumerate(
        [
            pool,
            blocks_of(fine_frame, PAD, NOWHERE),
            blocks_of(quads, PAD, NOWHERE),
            coarse_pool,
            blocks_of(coarse_frame, PAD, NOWHERE),
        ]
    ):
        by_row[at, : len(values)] = values
    by_column = np.full((720, 128), UNUSED, np.int32)
    for at, values in enumerate(
        [
            blocks_of(fine_frame, PAD, UNUSED),
            blocks_of(quads, PAD, UNUSED),
            blocks_of(coarse_frame, PAD, UNUSED),
            blocks_of([grid_places(range(6), range(12))], PAD, UNUSED),
            padded_codes(own, 288, UNUSED),
            padded_codes(grid_places(range(12), range(13, 24)), 144, UNUSED),
            padded_codes(grid_places(range(12), range(11)), 144, UNUSED),
            padded_codes(grid_places(range(7, 12), range(24)), 128, UNUSED),
            padded_codes(grid_places(range(5), range(24)), 128, UNUSED),
            padded_codes(grid_places(range(7, 12), sides), 112, UNUSED),
            padded_codes(grid_places(range(5), sides), 112, UNUSED),
            padded_codes(grid_places(range(1, 6), coarse_sides), 112, UNUSED),
            padded_codes(grid_places(range(5), coarse_sides), 112, UNUSED),
        ]
    ):
        by_column[: len(values), at] = values
    return by_row, by_column


def norm_rows(values, gain):
    middle = jnp.mean(values, axis=-1, keepdims=True)
    centered = values - middle
    spread = jnp.mean(centered * centered, axis=-1, keepdims=True)
    return centered * lax.rsqrt(spread + 1e-05) * gain


def dot(a, b):
    return jnp.dot(a, b, preferred_element_type=F32)


def dot_nt(a, b):
    return lax.dot_general(a, b, (((1,), (1,)), ((), ())), preferred_element_type=F32)


def kernel(
    shifts,
    fine_scale,
    coarse_scale,
    hbm_tokens,
    w_fine_qkv,
    w_fine_out,
    w_merge,
    w_coarse_qkv,
    w_coarse_out,
    hbm_fine_table,
    hbm_coarse_table,
    hbm_bias_index,
    hbm_fine_gain,
    hbm_merge_gain,
    hbm_coarse_gain,
    hbm_by_row,
    hbm_by_column,
    out,
    fine_qkv,
    fine_out,
    merge,
    coarse_qkv,
    coarse_out,
    pool,
    to_right,
    to_left,
    to_below,
    to_above,
    to_below_c,
    to_above_c,
    query,
    key,
    value,
    mixed,
    fine_after,
    coarse_pool,
    bias,
    tokens,
    fine_table,
    coarse_table,
    bias_index,
    fine_gain,
    merge_gain,
    coarse_gain,
    by_row,
    by_column,
    tables,
    to_below_k,
    to_above_k,
    send_sem,
    recv_sem,
    local_sem,
):
    lat, lon = lax.axis_index("lat"), lax.axis_index("lon")
    core, z_lo = lat % 2, lat // 2
    x, z_hi, y = lon // 8, (lon // 4) % 2, lon % 4
    z = z_hi * 8 + z_lo

    def place(x, y, z, core):
        x, y, z = (x + 4) % 4, (y + 4) % 4, (z + 16) % 16
        return ((z % 8) * 2 + core, x * 8 + (z // 8) * 4 + y)

    def along_z(d):
        return place(x, y, z + d, core)

    def along_x(d):
        return place(x + d, y, z, core)

    def along_y(d):
        return place(x, y + d, z, core)

    line = z * 2 + core

    def along_lat(d):
        spot = (line + d + 32) % 32
        return place(x, y, spot // 2, spot % 2)

    def along_lon(d):
        return (lat, (lon + d + 32) % 32)

    sibling = place(x, y, z, 1 - core)
    opposite = 4 - 8 * core
    hops = (opposite, 3, -3, 2, -2, 1, -1)

    barrier = pltpu.get_barrier_semaphore()
    senders = [along_z(-d) for d in hops]
    senders += [along_x(d) for d in (1, -1, 2)] + [along_y(d) for d in (1, -1, 2)]
    senders += [sibling, along_lon(1), along_lon(-1), along_lat(1), along_lat(-1)]
    for device in senders:
        pl.semaphore_signal(barrier, inc=1, device_id=device, device_id_type=MESH)

    local_count = [0]

    def bring(source, target):
        at = local_count[0]
        local_count[0] += 1
        copy = pltpu.make_async_copy(source, target, local_sem.at[at])
        copy.start()
        return copy

    first = [
        bring(hbm_tokens, tokens),
        bring(hbm_by_row, by_row),
        bring(hbm_by_column, by_column),
    ]
    later = [
        bring(hbm_fine_table, fine_table),
        bring(hbm_coarse_table, coarse_table),
        bring(hbm_bias_index, bias_index),
        bring(hbm_fine_gain, fine_gain),
        bring(hbm_merge_gain, merge_gain),
        bring(hbm_coarse_gain, coarse_gain),
    ]

    def picked(column, rows, row_at, first, width, offset=0):
        left = by_column[0:rows, column : column + 1] + offset
        right = by_row[row_at : row_at + 1, first : first + width]
        return jnp.where(left == right, 1.0, 0.0).astype(BF)

    counter = [0]
    sent = []

    def send(source, target, device):
        at = counter[0]
        counter[0] += 1
        copy = pltpu.make_async_remote_copy(
            src_ref=source,
            dst_ref=target,
            send_sem=send_sem.at[at],
            recv_sem=recv_sem.at[at],
            device_id=device,
            device_id_type=MESH,
        )
        copy.start()
        sent.append(copy)
        return copy

    def arrived(copies):
        for copy in copies:
            copy.wait_recv()

    class Gather:
        def __init__(self, shard, whole, halves):
            self.shard, self.whole, self.halves = shard, whole, halves

        def start(self):
            self.ready, self.waits = [], []
            for axis, part, pair_axis, small in self.halves:
                rows, columns = small
                source = self.shard.at[rows, columns]
                target = self.whole.at[z_lo, core, rows, columns]
                self.ready.append(bring(source, target))
                for d in hops:
                    self.waits.append(send(source, target, along_z(d)))

        def begun(self):
            for copy in self.ready:
                copy.wait()
            arrived(self.waits)
            self.ready, self.waits = [], []

        def pair(self):
            self.begun()
            for axis, part, pair_axis, (rows, columns) in self.halves:
                area = self.whole.at[:, core, rows, columns]
                self.waits.append(send(area, area, pair_axis(1)))

        def spread(self):
            self.begun()
            for axis, (rows, columns), pair_axis, small in self.halves:
                area = self.whole.at[:, core, rows, columns]
                for d in (1, -1, 2):
                    self.waits.append(send(area, area, axis(d)))

        def share(self):
            arrived(self.waits)
            part = self.whole.at[:, core]
            self.waits = [send(part, part, sibling)]

        def finish(self):
            arrived(self.waits)

    def by_x(part):
        return along_x, part(x), along_y, part(x, y % 2)

    def by_y(part):
        return along_y, part(y), along_x, part(y, x % 2)

    def corner(first, width):
        def part(g, half=None):
            rows = pl.ds(pl.multiple_of((g // 2) * 16, 16), 16)
            at, wide = first + (g % 2) * width, width
            if half is not None:
                at, wide = at + half * (width // 2), width // 2
            return rows, pl.ds(pl.multiple_of(at, 128), wide)

        return part

    def band(first, width):
        def part(g, half=None):
            if half is None:
                return pl.ds(pl.multiple_of(g * 32, 32), 32), pl.ds(first, width)
            return pl.ds(pl.multiple_of(g * 32 + half * 16, 16), 16), pl.ds(first, width)

        return part

    def quarters(axis, g, first):
        part = corner(first, 384)(g)
        return axis, part, None, part

    g_fine_qkv = Gather(
        w_fine_qkv, fine_qkv, [quarters(along_x, x, 0), quarters(along_y, y, 768)]
    )
    g_fine_out = Gather(w_fine_out, fine_out, [by_x(corner(0, 256))])
    g_merge = Gather(w_merge, merge, [by_x(band(0, 256)), by_y(band(256, 256))])
    g_coarse_qkv = Gather(w_coarse_qkv, coarse_qkv, [by_x(corner(0, 768))])
    g_coarse_out = Gather(w_coarse_out, coarse_out, [by_y(corner(0, 256))])

    pl.semaphore_wait(barrier, len(senders))
    g_fine_qkv.start()
    g_fine_out.start()
    g_merge.start()
    for copy in first:
        copy.wait()
    own = tokens[...]
    to_right[...] = dot(picked(5, 144, 0, OWN, 288), own).astype(BF)
    to_left[...] = dot(picked(6, 144, 0, OWN, 288), own).astype(BF)
    to_below[...] = dot(picked(7, 128, 0, OWN, 288), own).astype(BF)
    to_above[...] = dot(picked(8, 128, 0, OWN, 288), own).astype(BF)
    pool[OWN : OWN + 288, :] = own

    bias[...] = jnp.zeros((16, PAD, 128), F32)
    tables[...] = jnp.zeros((16, 256), F32)
    for copy in later:
        copy.wait()
    tables[0:HEADS, 0:253] = fine_table[...]
    tables[HEADS : 2 * HEADS, 0:253] = coarse_table[...]
    table = tables[...]
    top = table.astype(BF)
    rest = table - top.astype(F32)
    middle = rest.astype(BF)
    bottom = (rest - middle.astype(F32)).astype(BF)
    table_parts = jnp.concatenate([top, middle, bottom], axis=0)
    levels = lax.broadcasted_iota(jnp.int32, (256, WIN), 0)

    def bias_rows(group, carry):
        rows = bias_index[pl.ds(pl.multiple_of(group * 8, 8), 8), :]
        for i in range(8):
            hot = jnp.where(levels == rows[i : i + 1, :], 1.0, 0.0).astype(BF)
            parts = dot(table_parts, hot)
            looked = parts[0:16] + parts[16:32] + parts[32:48]
            bias[:, pl.ds(group * 8 + i, 1), 0:WIN] = looked.reshape(16, 1, WIN)
        return carry

    lax.fori_loop(0, WIN // 8, bias_rows, 0)

    g_fine_qkv.spread()
    side_copies = [
        send(to_right, pool.at[pl.ds(LEFT, 144)], along_lon(1)),
        send(to_left, pool.at[pl.ds(RIGHT, 144)], along_lon(-1)),
    ]
    row_copies = [
        send(to_below, pool.at[pl.ds(ABOVE, 128)], along_lat(1)),
        send(to_above, pool.at[pl.ds(BELOW, 128)], along_lat(-1)),
    ]
    g_fine_qkv.share()
    g_fine_out.pair()
    g_merge.pair()

    lane = lax.broadcasted_iota(jnp.int32, (1, 128), 1)
    low = jnp.where(lane < 64, 1.0, 0.0).astype(BF)
    high = jnp.where(lane < 64, 0.0, 1.0).astype(BF)
    row_of = jnp.zeros((1, 128), jnp.int32)
    for r in range(1, WLAT):
        row_of = row_of + jnp.where(lane >= WLON * r, 1, 0)
    ones_row = lax.broadcasted_iota(jnp.int32, (256, 256), 0) // 64
    ones_column = lax.broadcasted_iota(jnp.int32, (256, 256), 1) // 64
    same_head = jnp.where(ones_row == ones_column, 1.0, 0.0).astype(BF)

    def scale_row(scale):
        head_of = lax.broadcasted_iota(jnp.int32, (1, D), 1) // 64
        row = jnp.zeros((1, D), F32)
        for n in range(HEADS):
            row = jnp.where(head_of == n, scale[n], row)
        return row

    def project(level, windows, column, row_at, cells, first, width, weights, scale):
        offset = shifts[level, 0] * 128 + shifts[level, 1]
        scales = scale_row(scale)
        at, count = windows
        left = by_column[at * PAD : (at + count) * PAD, column : column + 1] + offset
        right = by_row[row_at : row_at + 1, first : first + width]
        hot = jnp.where(left == right, 1.0, 0.0).astype(BF)
        frame = dot(hot, cells[first : first + width, :]).astype(BF)
        for n in range(6):
            block = weights[:, :, :, 256 * n : 256 * n + 256].reshape(D, 256)
            rounded = dot(frame, block).astype(BF)
            columns = slice(256 * (n % 2), 256 * (n % 2) + 256)
            if n < 4:
                full = rounded.astype(F32)
                square = dot((full * full).astype(BF), same_head)
                full = full * lax.rsqrt(square + 1e-06)
                if n < 2:
                    full = full * scales[:, columns]
                rounded = full.astype(BF)
            target = (query, key, value)[n // 2]
            target[at : at + count, :, columns] = rounded.reshape(count, PAD, 256)

    def attend(level, windows, row_block, rows_here):
        first_row = lat * rows_here + shifts[level, 0] - WLAT
        at, count = windows

        def one(w, carry):
            latitude = row_of + (first_row + WLAT * row_block(w))
            here = (latitude >= 0) & (latitude < rows_here * 16) & (lane < WIN)
            keep = jnp.where(here, 1.0, 0.0)[:, 0:PAD]
            for p in range(HEADS // 2):
                columns = slice(128 * p, 128 * p + 128)
                q = query[at + w, :, columns]
                pair = jnp.concatenate([q * low, q * high], axis=0)
                scores = dot_nt(pair, key[at + w, :, columns])
                own_bias = bias[8 * level + 2 * p : 8 * level + 2 * p + 2, :, 0:PAD]
                powers = jnp.exp(scores + own_bias.reshape(2 * PAD, PAD)) * keep
                total = jnp.sum(powers, axis=-1, keepdims=True)
                weights = (powers * (1.0 / total)).astype(BF)
                both = dot(weights, value[at + w, :, columns])
                taken = jnp.where(lane < 64, both[0:PAD], both[PAD : 2 * PAD])
                mixed[at + w, :, columns] = taken.astype(BF)
            return carry

        lax.fori_loop(0, count, one, 0)

    def finish(level, windows, column, rows, row_at, weights, base, gain):
        offset = shifts[level, 0] * 128 + shifts[level, 1]
        left = by_column[0:rows, column : column + 1] - offset
        right = by_row[row_at : row_at + 1, 0 : windows * PAD]
        hot = jnp.where(left == right, 1.0, 0.0).astype(BF)
        taken = dot(hot, mixed[0:windows].reshape(windows * PAD, D)).astype(BF)
        branch = dot(taken, weights[...].reshape(D, D))
        return (base + norm_rows(branch, gain)).astype(BF)

    g_fine_qkv.finish()
    arrived(row_copies)
    project(0, (0, 3), 0, 0, pool, ABOVE, 544, fine_qkv, fine_scale)
    g_fine_out.spread()
    g_merge.spread()
    attend(0, (0, 3), lambda w: w, 12)

    arrived(side_copies)
    near = pool[OWN : OWN + 576, :]
    to_below_c[...] = dot(picked(9, 112, 0, OWN, 576), near).astype(BF)
    to_above_c[...] = dot(picked(10, 112, 0, OWN, 576), near).astype(BF)
    row_copies = [
        send(to_below_c, pool.at[pl.ds(ABOVE_C, 112)], along_lat(1)),
        send(to_above_c, pool.at[pl.ds(BELOW_C, 112)], along_lat(-1)),
    ]
    g_coarse_qkv.start()
    g_coarse_out.start()
    project(0, (3, 2), 0, 0, pool, OWN, 576, fine_qkv, fine_scale)
    attend(0, (3, 2), lambda w: 1, 12)

    arrived(row_copies)
    project(0, (5, 4), 0, 0, pool, 0, POOL, fine_qkv, fine_scale)
    g_fine_out.share()
    attend(0, (5, 4), lambda w: 2 * (w // 2), 12)
    g_merge.share()
    g_fine_out.finish()
    in_quads = dot(picked(1, 320, 0, OWN, 288), tokens[...])
    fine_after[...] = finish(0, 9, 1, 320, 1, fine_out, in_quads, fine_gain[...])
    g_coarse_qkv.pair()
    g_coarse_out.pair()
    g_merge.finish()
    merged = jnp.zeros((PAD, D), F32)
    for p in range(4):
        rows = merge[2 * p : 2 * p + 2].reshape(D, D)
        merged = merged + dot(fine_after[PAD * p : PAD * p + PAD, :], rows)
    coarse_pool[0:PAD, :] = norm_rows(merged, merge_gain[...]).astype(BF)
    mine = coarse_pool.at[pl.ds(0, PAD)]
    side_copies = [
        send(mine, coarse_pool.at[pl.ds(C_LEFT, PAD)], along_lon(1)),
        send(mine, coarse_pool.at[pl.ds(C_RIGHT, PAD)], along_lon(-1)),
    ]
    row_copies = [
        send(mine, coarse_pool.at[pl.ds(C_ABOVE, PAD)], along_lat(1)),
        send(mine, coarse_pool.at[pl.ds(C_BELOW, PAD)], along_lat(-1)),
    ]
    g_coarse_qkv.spread()
    g_coarse_out.spread()
    arrived(side_copies)
    near = coarse_pool[0 : 3 * PAD, :]
    to_below_k[...] = dot(picked(11, 112, 3, 0, 3 * PAD), near).astype(BF)
    to_above_k[...] = dot(picked(12, 112, 3, 0, 3 * PAD), near).astype(BF)
    row_copies += [
        send(to_below_k, coarse_pool.at[pl.ds(C_ABOVE_C, 112)], along_lat(1)),
        send(to_above_k, coarse_pool.at[pl.ds(C_BELOW_C, 112)], along_lat(-1)),
    ]
    g_coarse_qkv.share()
    g_coarse_out.share()
    g_coarse_qkv.finish()
    arrived(row_copies)
    project(1, (0, 4), 2, 3, coarse_pool, 0, CPOOL, coarse_qkv, coarse_scale)
    attend(1, (0, 4), lambda w: w // 2, 6)
    g_coarse_out.finish()
    base = coarse_pool[0:PAD, :].astype(F32)
    coarse_after = finish(1, 4, 3, PAD, 4, coarse_out, base, coarse_gain[...]).astype(F32)
    for p in range(4):
        part = fine_after[PAD * p : PAD * p + PAD, :].astype(F32) + coarse_after
        fine_after[PAD * p : PAD * p + PAD, :] = part.astype(BF)
    out[...] = dot(picked(4, 288, 2, 0, 320), fine_after[...]).astype(BF)
    for copy in sent:
        copy.wait_send()


COPIES = 12 + 21 + 12 + 23 + 12 + 12


def per_device(
    tokens,
    fine_qkv,
    fine_out,
    fine_scale,
    fine_table,
    fine_gain,
    merge_weight,
    merge_gain,
    coarse_qkv,
    coarse_out,
    coarse_scale,
    coarse_table,
    coarse_gain,
    shifts,
    bias_index,
):
    by_row, by_column = code_tables()
    rows, columns, width = tokens.shape
    smem = pl.BlockSpec(memory_space=pltpu.SMEM)
    vmem = pl.BlockSpec(memory_space=pltpu.VMEM)
    hbm = pl.BlockSpec(memory_space=pltpu.HBM)
    result = pl.pallas_call(
        kernel,
        out_shape=jax.ShapeDtypeStruct((rows * columns, width), BF),
        in_specs=[smem] * 3 + [hbm] * 14,
        out_specs=vmem,
        scratch_shapes=[
            pltpu.VMEM((8, 2, 32, 1536), BF),
            pltpu.VMEM((8, 2, 32, 512), BF),
            pltpu.VMEM((8, 2, 128, 512), BF),
            pltpu.VMEM((8, 2, 32, 1536), BF),
            pltpu.VMEM((8, 2, 32, 512), BF),
            pltpu.VMEM((POOL, D), BF),
            pltpu.VMEM((144, D), BF),
            pltpu.VMEM((144, D), BF),
            pltpu.VMEM((128, D), BF),
            pltpu.VMEM((128, D), BF),
            pltpu.VMEM((112, D), BF),
            pltpu.VMEM((112, D), BF),
            pltpu.VMEM((9, PAD, D), BF),
            pltpu.VMEM((9, PAD, D), BF),
            pltpu.VMEM((9, PAD, D), BF),
            pltpu.VMEM((9, PAD, D), BF),
            pltpu.VMEM((320, D), BF),
            pltpu.VMEM((CPOOL, D), BF),
            pltpu.VMEM((16, PAD, 128), F32),
            pltpu.VMEM((288, D), BF),
            pltpu.VMEM((HEADS, 253), F32),
            pltpu.VMEM((HEADS, 253), F32),
            pltpu.VMEM((WIN, WIN), jnp.int32),
            pltpu.VMEM((1, D), F32),
            pltpu.VMEM((1, D), F32),
            pltpu.VMEM((1, D), F32),
            pltpu.VMEM((8, 1152), jnp.int32),
            pltpu.VMEM((720, 128), jnp.int32),
            pltpu.VMEM((16, 256), F32),
            pltpu.VMEM((112, D), BF),
            pltpu.VMEM((112, D), BF),
            pltpu.SemaphoreType.DMA((COPIES,)),
            pltpu.SemaphoreType.DMA((COPIES,)),
            pltpu.SemaphoreType.DMA((20,)),
        ],
        compiler_params=pltpu.CompilerParams(
            collective_id=0, has_side_effects=True, vmem_limit_bytes=64 << 20
        ),
    )(
        shifts,
        fine_scale,
        coarse_scale,
        tokens.reshape(rows * columns, width),
        fine_qkv,
        fine_out,
        merge_weight,
        coarse_qkv,
        coarse_out,
        fine_table.T,
        coarse_table.T,
        bias_index,
        fine_gain.reshape(1, -1),
        merge_gain.reshape(1, -1),
        coarse_gain.reshape(1, -1),
        jnp.asarray(by_row),
        jnp.asarray(by_column),
    )
    return result.reshape(rows, columns, width)


def solution(mesh):
    placed = (
        P("lat", "lon", None),
        P("lat", None),
        P("lat", None),
        P(),
        P(),
        P(),
        P("lat", None),
        P(),
        P("lat", None),
        P("lat", None),
        P(),
        P(),
        P(),
        P(),
        P(),
    )
    return jax.shard_map(
        per_device, mesh=mesh, in_specs=placed, out_specs=P("lat", "lon", None), check_vma=False
    )
```

time: 103 us -> 86.7 us (0.84)
  Pallas kernels: 93.1 us -> 84.8 us
  local copies, waits for them, and re-layouts: 7.55 us -> 1.69 us
  other arithmetic: 1.49 us -> 0 us
    pallas_call x1, Pallas kernels: 93.1 us -> 84.8 us  [per_device(): pl.pallas_call(kernel, out_shape=jax.ShapeDtypeStruct((rows * columns, wi...]
    unnamed x23 -> x1, local copies, waits for them, and re-layouts: 6.74 us -> 1.69 us
where the time goes in v2:
time: 86.7 us; the launch traced here: 86.5 us
  Pallas kernels  84.8 us (98%)
  local copies, waits for them, and re-layouts  1.69 us (2%)
    pallas_call x1, Pallas kernels, per_device(): pl.pallas_call(kernel, out_shape=jax.ShapeDtypeStruct((rows * columns, wi...  84.8 us

profile of v2, /device:TPU:1, one launch (start us, length us, event | category | flops | bytes accessed | tf_op | source)
XLA Modules:
  0.0 86.5 jit_solution(16418796004135296417)
XLA Ops:
  0.0 84.8 %shard_map.163 = bf16[288,512]{1,0:T(8,128)(2,1)} custom-call(s32[2,2]{1,0:T(2,128)} %shifts.1, f32[8]{0:T(128)} %fine_scale.1, f32[8]{0:T(128)} %coarse_scale.1, bf16[288,512]{1,0:T(8,128)(2,1)} %bitcast.8, bf16[32,1536]{1,0:T(8,128)(2,1)} %w_fine_qkv.1, bf16[32,512]{1,0:T(8,128)(2,1)} %w_fine_out.1, bf16[128,512]{1,0:T(8,128)(2,1)} %w_merge.1, ...), custom_call_target="tpu_custom_call" | custom-call | tf_op jit(solution)/shard_map/pallas_call | solution.py:582
  84.8 1.7 %copy.19 = bf16[12,24,512]{2,1,0:T(8,128)(2,1)} copy(bf16[12,24,512]{2,1,0:T(8,128)(2,1)} %bitcast.7) | data formatting | bytes 589824

commit v3 on v2

--- a/solution.py
+++ b/solution.py
@@ -24,6 +24,7 @@
 CPOOL = 624
 FINE_WINDOWS = [(0, 1), (1, 1), (2, 1), (1, 0), (1, 2), (0, 0), (0, 2), (2, 0), (2, 2)]
 COARSE_WINDOWS = [(0, 0), (0, 1), (1, 0), (1, 1)]
+LOG2E = 1.4426950408889634
 NOWHERE = -200000
 UNUSED = -100000
 
@@ -372,6 +373,15 @@
     to_above[...] = dot(picked(8, 128, 0, OWN, 288), own).astype(BF)
     pool[OWN : OWN + 288, :] = own
 
+    g_fine_qkv.spread()
+    side_copies = [
+        send(to_right, pool.at[pl.ds(LEFT, 144)], along_lon(1)),
+        send(to_left, pool.at[pl.ds(RIGHT, 144)], along_lon(-1)),
+    ]
+    row_copies = [
+        send(to_below, pool.at[pl.ds(ABOVE, 128)], along_lat(1)),
+        send(to_above, pool.at[pl.ds(BELOW, 128)], along_lat(-1)),
+    ]
     bias[...] = jnp.zeros((16, PAD, 128), F32)
     tables[...] = jnp.zeros((16, 256), F32)
     for copy in later:
@@ -391,21 +401,12 @@
         for i in range(8):
             hot = jnp.where(levels == rows[i : i + 1, :], 1.0, 0.0).astype(BF)
             parts = dot(table_parts, hot)
-            looked = parts[0:16] + parts[16:32] + parts[32:48]
+            looked = (parts[0:16] + parts[16:32] + parts[32:48]) * LOG2E
             bias[:, pl.ds(group * 8 + i, 1), 0:WIN] = looked.reshape(16, 1, WIN)
         return carry
 
     lax.fori_loop(0, WIN // 8, bias_rows, 0)
 
-    g_fine_qkv.spread()
-    side_copies = [
-        send(to_right, pool.at[pl.ds(LEFT, 144)], along_lon(1)),
-        send(to_left, pool.at[pl.ds(RIGHT, 144)], along_lon(-1)),
-    ]
-    row_copies = [
-        send(to_below, pool.at[pl.ds(ABOVE, 128)], along_lat(1)),
-        send(to_above, pool.at[pl.ds(BELOW, 128)], along_lat(-1)),
-    ]
     g_fine_qkv.share()
     g_fine_out.pair()
     g_merge.pair()
@@ -413,9 +414,10 @@
     lane = lax.broadcasted_iota(jnp.int32, (1, 128), 1)
     low = jnp.where(lane < 64, 1.0, 0.0).astype(BF)
     high = jnp.where(lane < 64, 0.0, 1.0).astype(BF)
-    row_of = jnp.zeros((1, 128), jnp.int32)
+    position = lax.broadcasted_iota(jnp.int32, (PAD, 128), 0)
+    row_of = jnp.zeros((PAD, 128), jnp.int32)
     for r in range(1, WLAT):
-        row_of = row_of + jnp.where(lane >= WLON * r, 1, 0)
+        row_of = row_of + jnp.where(position >= WLON * r, 1, 0)
     ones_row = lax.broadcasted_iota(jnp.int32, (256, 256), 0) // 64
     ones_column = lax.broadcasted_iota(jnp.int32, (256, 256), 1) // 64
     same_head = jnp.where(ones_row == ones_column, 1.0, 0.0).astype(BF)
@@ -424,17 +426,21 @@
         head_of = lax.broadcasted_iota(jnp.int32, (1, D), 1) // 64
         row = jnp.zeros((1, D), F32)
         for n in range(HEADS):
-            row = jnp.where(head_of == n, scale[n], row)
+            row = jnp.where(head_of == n, scale[n] * LOG2E, row)
         return row
 
-    def project(level, windows, column, row_at, cells, first, width, weights, scale):
+    def framed(level, windows, column, row_at, cells, first, width):
         offset = shifts[level, 0] * 128 + shifts[level, 1]
-        scales = scale_row(scale)
         at, count = windows
         left = by_column[at * PAD : (at + count) * PAD, column : column + 1] + offset
         right = by_row[row_at : row_at + 1, first : first + width]
         hot = jnp.where(left == right, 1.0, 0.0).astype(BF)
-        frame = dot(hot, cells[first : first + width, :]).astype(BF)
+        return dot(hot, cells[first : first + width, :])
+
+    def project(windows, cells, weights, scale):
+        scales = scale_row(scale)
+        at, count = windows
+        frame = cells.astype(BF)
         for n in range(6):
             block = weights[:, :, :, 256 * n : 256 * n + 256].reshape(D, 256)
             rounded = dot(frame, block).astype(BF)
@@ -455,23 +461,24 @@
 
         def one(w, carry):
             latitude = row_of + (first_row + WLAT * row_block(w))
-            here = (latitude >= 0) & (latitude < rows_here * 16) & (lane < WIN)
-            keep = jnp.where(here, 1.0, 0.0)[:, 0:PAD]
+            here = (latitude >= 0) & (latitude < rows_here * 16) & (position < WIN)
+            keep = jnp.where(here, 1.0, 0.0).astype(BF)
             for p in range(HEADS // 2):
                 columns = slice(128 * p, 128 * p + 128)
                 q = query[at + w, :, columns]
                 pair = jnp.concatenate([q * low, q * high], axis=0)
                 scores = dot_nt(pair, key[at + w, :, columns])
                 own_bias = bias[8 * level + 2 * p : 8 * level + 2 * p + 2, :, 0:PAD]
-                powers = jnp.exp(scores + own_bias.reshape(2 * PAD, PAD)) * keep
-                total = jnp.sum(powers, axis=-1, keepdims=True)
-                weights = (powers * (1.0 / total)).astype(BF)
-                both = dot(weights, value[at + w, :, columns])
-                taken = jnp.where(lane < 64, both[0:PAD], both[PAD : 2 * PAD])
+                powers = jnp.exp2(scores + own_bias.reshape(2 * PAD, PAD)).astype(BF)
+                kept = jnp.concatenate([value[at + w, :, columns] * keep, keep], axis=1)
+                both = dot(powers, kept)
+                mine = jnp.where(lane < 64, both[0:PAD, 0:128], both[PAD : 2 * PAD, 0:128])
+                total = jnp.where(lane < 64, both[0:PAD, 128:256], both[PAD : 2 * PAD, 128:256])
+                taken = mine / total
                 mixed[at + w, :, columns] = taken.astype(BF)
             return carry
 
-        lax.fori_loop(0, count, one, 0)
+        lax.fori_loop(0, count, one, 0, unroll=True)
 
     def finish(level, windows, column, rows, row_at, weights, base, gain):
         offset = shifts[level, 0] * 128 + shifts[level, 1]
@@ -484,7 +491,8 @@
 
     g_fine_qkv.finish()
     arrived(row_copies)
-    project(0, (0, 3), 0, 0, pool, ABOVE, 544, fine_qkv, fine_scale)
+    frame = framed(0, (0, 3), 0, 0, pool, ABOVE, 544)
+    project((0, 3), frame, fine_qkv, fine_scale)
     g_fine_out.spread()
     g_merge.spread()
     attend(0, (0, 3), lambda w: w, 12)
@@ -499,11 +507,14 @@
     ]
     g_coarse_qkv.start()
     g_coarse_out.start()
-    project(0, (3, 2), 0, 0, pool, OWN, 576, fine_qkv, fine_scale)
+    frame = framed(0, (3, 2), 0, 0, pool, OWN, 576)
+    project((3, 2), frame, fine_qkv, fine_scale)
     attend(0, (3, 2), lambda w: 1, 12)
 
+    frame = framed(0, (5, 4), 0, 0, pool, 0, ABOVE_C)
     arrived(row_copies)
-    project(0, (5, 4), 0, 0, pool, 0, POOL, fine_qkv, fine_scale)
+    frame = frame + framed(0, (5, 4), 0, 0, pool, ABOVE_C, POOL - ABOVE_C)
+    project((5, 4), frame, fine_qkv, fine_scale)
     g_fine_out.share()
     attend(0, (5, 4), lambda w: 2 * (w // 2), 12)
     g_merge.share()
@@ -539,9 +550,14 @@
     ]
     g_coarse_qkv.share()
     g_coarse_out.share()
+    frame = framed(1, (0, 4), 2, 3, coarse_pool, 0, C_ABOVE)
     g_coarse_qkv.finish()
-    arrived(row_copies)
-    project(1, (0, 4), 2, 3, coarse_pool, 0, CPOOL, coarse_qkv, coarse_scale)
+    arrived(row_copies[:2])
+    frame = frame + framed(1, (0, 4), 2, 3, coarse_pool, C_ABOVE, C_ABOVE_C - C_ABOVE)
+    arrived(row_copies[2:])
+    corners = CPOOL - C_ABOVE_C
+    frame = frame + framed(1, (0, 4), 2, 3, coarse_pool, C_ABOVE_C, corners)
+    project((0, 4), frame, coarse_qkv, coarse_scale)
     attend(1, (0, 4), lambda w: w // 2, 6)
     g_coarse_out.finish()
     base = coarse_pool[0:PAD, :].astype(F32)

time: 86.7 us -> 85.3 us (0.984)
  Pallas kernels: 84.8 us -> 83.4 us
    pallas_call x1, Pallas kernels: 84.8 us -> 83.4 us  [per_device(): pl.pallas_call(kernel, out_shape=jax.ShapeDtypeStruct((rows * columns, wi...]
where the time goes in v3:
time: 85.3 us; the launch traced here: 85.1 us
  Pallas kernels  83.4 us (98%)
  local copies, waits for them, and re-layouts  1.69 us (2%)
    pallas_call x1, Pallas kernels, per_device(): pl.pallas_call(kernel, out_shape=jax.ShapeDtypeStruct((rows * columns, wi...  83.4 us

profile of v3, /device:TPU:1, one launch (start us, length us, event | category | flops | bytes accessed | tf_op | source)
XLA Modules:
  0.0 85.1 jit_solution(18196058023112211244)
XLA Ops:
  0.0 83.4 %shard_map.163 = bf16[288,512]{1,0:T(8,128)(2,1)} custom-call(s32[2,2]{1,0:T(2,128)} %shifts.1, f32[8]{0:T(128)} %fine_scale.1, f32[8]{0:T(128)} %coarse_scale.1, bf16[288,512]{1,0:T(8,128)(2,1)} %bitcast.8, bf16[32,1536]{1,0:T(8,128)(2,1)} %w_fine_qkv.1, bf16[32,512]{1,0:T(8,128)(2,1)} %w_fine_out.1, bf16[128,512]{1,0:T(8,128)(2,1)} %w_merge.1, ...), custom_call_target="tpu_custom_call" | custom-call | tf_op jit(solution)/shard_map/pallas_call | solution.py:598
  83.4 1.7 %copy.19 = bf16[12,24,512]{2,1,0:T(8,128)(2,1)} copy(bf16[12,24,512]{2,1,0:T(8,128)(2,1)} %bitcast.7) | data formatting | bytes 589824

commit v4 on v3

--- a/solution.py
+++ b/solution.py
@@ -490,11 +490,11 @@
         return (base + norm_rows(branch, gain)).astype(BF)
 
     g_fine_qkv.finish()
+    g_fine_out.spread()
+    g_merge.spread()
     arrived(row_copies)
     frame = framed(0, (0, 3), 0, 0, pool, ABOVE, 544)
     project((0, 3), frame, fine_qkv, fine_scale)
-    g_fine_out.spread()
-    g_merge.spread()
     attend(0, (0, 3), lambda w: w, 12)
 
     arrived(side_copies)
@@ -514,10 +514,10 @@
     frame = framed(0, (5, 4), 0, 0, pool, 0, ABOVE_C)
     arrived(row_copies)
     frame = frame + framed(0, (5, 4), 0, 0, pool, ABOVE_C, POOL - ABOVE_C)
+    g_fine_out.share()
+    g_merge.share()
     project((5, 4), frame, fine_qkv, fine_scale)
-    g_fine_out.share()
     attend(0, (5, 4), lambda w: 2 * (w // 2), 12)
-    g_merge.share()
     g_fine_out.finish()
     in_quads = dot(picked(1, 320, 0, OWN, 288), tokens[...])
     fine_after[...] = finish(0, 9, 1, 320, 1, fine_out, in_quads, fine_gain[...])

time: 85.3 us -> 84.2 us (0.987)
  Pallas kernels: 83.4 us -> 82.3 us
    pallas_call x1, Pallas kernels: 83.4 us -> 82.3 us  [per_device(): pl.pallas_call(kernel, out_shape=jax.ShapeDtypeStruct((rows * columns, wi...]
where the time goes in v4:
time: 84.2 us; the launch traced here: 84 us
  Pallas kernels  82.3 us (98%)
  local copies, waits for them, and re-layouts  1.69 us (2%)
    pallas_call x1, Pallas kernels, per_device(): pl.pallas_call(kernel, out_shape=jax.ShapeDtypeStruct((rows * columns, wi...  82.3 us
    unnamed x1, local copies, waits for them, and re-layouts  1.69 us

profile of v4, /device:TPU:1, one launch (start us, length us, event | category | flops | bytes accessed | tf_op | source)
XLA Modules:
  0.0 84.0 jit_solution(2492180558678080287)
XLA Ops:
  0.0 82.3 %shard_map.163 = bf16[288,512]{1,0:T(8,128)(2,1)} custom-call(s32[2,2]{1,0:T(2,128)} %shifts.1, f32[8]{0:T(128)} %fine_scale.1, f32[8]{0:T(128)} %coarse_scale.1, bf16[288,512]{1,0:T(8,128)(2,1)} %bitcast.8, bf16[32,1536]{1,0:T(8,128)(2,1)} %w_fine_qkv.1, bf16[32,512]{1,0:T(8,128)(2,1)} %w_fine_out.1, bf16[128,512]{1,0:T(8,128)(2,1)} %w_merge.1, ...), custom_call_target="tpu_custom_call" | custom-call | tf_op jit(solution)/shard_map/pallas_call | solution.py:598
  82.3 1.7 %copy.19 = bf16[12,24,512]{2,1,0:T(8,128)(2,1)} copy(bf16[12,24,512]{2,1,0:T(8,128)(2,1)} %bitcast.7) | data formatting | bytes 589824

commit v5 on v4

--- a/solution.py
+++ b/solution.py
@@ -505,11 +505,11 @@
         send(to_below_c, pool.at[pl.ds(ABOVE_C, 112)], along_lat(1)),
         send(to_above_c, pool.at[pl.ds(BELOW_C, 112)], along_lat(-1)),
     ]
-    g_coarse_qkv.start()
-    g_coarse_out.start()
     frame = framed(0, (3, 2), 0, 0, pool, OWN, 576)
     project((3, 2), frame, fine_qkv, fine_scale)
     attend(0, (3, 2), lambda w: 1, 12)
+    g_coarse_qkv.start()
+    g_coarse_out.start()
 
     frame = framed(0, (5, 4), 0, 0, pool, 0, ABOVE_C)
     arrived(row_copies)

time: 84.2 us -> 85.1 us (1.011)
  Pallas kernels: 82.3 us -> 83.2 us
    pallas_call x1, Pallas kernels: 82.3 us -> 83.2 us  [per_device(): pl.pallas_call(kernel, out_shape=jax.ShapeDtypeStruct((rows * columns, wi...]
where the time goes in v5:
time: 85.1 us; the launch traced here: 84.9 us
  Pallas kernels  83.2 us (98%)
  local copies, waits for them, and re-layouts  1.69 us (2%)
    pallas_call x1, Pallas kernels, per_device(): pl.pallas_call(kernel, out_shape=jax.ShapeDtypeStruct((rows * columns, wi...  83.2 us

profile of v5, /device:TPU:1, one launch (start us, length us, event | category | flops | bytes accessed | tf_op | source)
XLA Modules:
  0.0 84.9 jit_solution(4807245657349839271)
XLA Ops:
  0.0 83.2 %shard_map.163 = bf16[288,512]{1,0:T(8,128)(2,1)} custom-call(s32[2,2]{1,0:T(2,128)} %shifts.1, f32[8]{0:T(128)} %fine_scale.1, f32[8]{0:T(128)} %coarse_scale.1, bf16[288,512]{1,0:T(8,128)(2,1)} %bitcast.8, bf16[32,1536]{1,0:T(8,128)(2,1)} %w_fine_qkv.1, bf16[32,512]{1,0:T(8,128)(2,1)} %w_fine_out.1, bf16[128,512]{1,0:T(8,128)(2,1)} %w_merge.1, ...), custom_call_target="tpu_custom_call" | custom-call | tf_op jit(solution)/shard_map/pallas_call | solution.py:598
  83.2 1.7 %copy.19 = bf16[12,24,512]{2,1,0:T(8,128)(2,1)} copy(bf16[12,24,512]{2,1,0:T(8,128)(2,1)} %bitcast.7) | data formatting | bytes 589824

commit v6 on v4

--- a/solution.py
+++ b/solution.py
@@ -517,12 +517,14 @@
     g_fine_out.share()
     g_merge.share()
     project((5, 4), frame, fine_qkv, fine_scale)
+    g_coarse_qkv.pair()
+    g_coarse_out.pair()
     attend(0, (5, 4), lambda w: 2 * (w // 2), 12)
     g_fine_out.finish()
     in_quads = dot(picked(1, 320, 0, OWN, 288), tokens[...])
     fine_after[...] = finish(0, 9, 1, 320, 1, fine_out, in_quads, fine_gain[...])
-    g_coarse_qkv.pair()
-    g_coarse_out.pair()
+    g_coarse_qkv.spread()
+    g_coarse_out.spread()
     g_merge.finish()
     merged = jnp.zeros((PAD, D), F32)
     for p in range(4):
@@ -538,8 +540,6 @@
         send(mine, coarse_pool.at[pl.ds(C_ABOVE, PAD)], along_lat(1)),
         send(mine, coarse_pool.at[pl.ds(C_BELOW, PAD)], along_lat(-1)),
     ]
-    g_coarse_qkv.spread()
-    g_coarse_out.spread()
     arrived(side_copies)
     near = coarse_pool[0 : 3 * PAD, :]
     to_below_k[...] = dot(picked(11, 112, 3, 0, 3 * PAD), near).astype(BF)

time: 84.2 us -> 85.3 us (1.013); the launches traced: 84 us -> 83.8 us
  no operation moved by 1% of the time
where the time goes in v6:
time: 85.3 us; the launch traced here: 83.8 us
  Pallas kernels  82.1 us (96%)
  local copies, waits for them, and re-layouts  1.69 us (2%)
    pallas_call x1, Pallas kernels, per_device(): pl.pallas_call(kernel, out_shape=jax.ShapeDtypeStruct((rows * columns, wi...  82.1 us

profile of v6, /device:TPU:1, one launch (start us, length us, event | category | flops | bytes accessed | tf_op | source)
XLA Modules:
  0.0 83.8 jit_solution(726218921843021032)
XLA Ops:
  0.0 82.1 %shard_map.163 = bf16[288,512]{1,0:T(8,128)(2,1)} custom-call(s32[2,2]{1,0:T(2,128)} %shifts.1, f32[8]{0:T(128)} %fine_scale.1, f32[8]{0:T(128)} %coarse_scale.1, bf16[288,512]{1,0:T(8,128)(2,1)} %bitcast.8, bf16[32,1536]{1,0:T(8,128)(2,1)} %w_fine_qkv.1, bf16[32,512]{1,0:T(8,128)(2,1)} %w_fine_out.1, bf16[128,512]{1,0:T(8,128)(2,1)} %w_merge.1, ...), custom_call_target="tpu_custom_call" | custom-call | tf_op jit(solution)/shard_map/pallas_call | solution.py:598
  82.1 1.7 %copy.19 = bf16[12,24,512]{2,1,0:T(8,128)(2,1)} copy(bf16[12,24,512]{2,1,0:T(8,128)(2,1)} %bitcast.7) | data formatting | bytes 589824
